TPU v7x, 512 devices: a whole 4x8x8 slice. The times are simulated.
512 devices in a mesh: pairs: 64 (over z, y_hi, x), dims: 8 (over y_lo, core).
Axes of the slice: x: 4, y: 8 (y_hi: 2, y_lo: 4; y = y_hi * 4 + y_lo), z: 8, core: 2. Of those that a mesh axis runs over, the one named last changes fastest.
Arguments:
- first_view: bfloat16 [8192, 4096], P('pairs', 'dims'), may hold values from -40 to 40
- second_view: bfloat16 [8192, 4096], P('pairs', 'dims'), may hold values from -40 to 40
- weight: bfloat16 [4096, 4096], P(None, 'dims'), may hold values from -0.09375 to 0.09375
- pre_act: bfloat16 [8192, 4096], P('pairs', 'dims'), may hold values from -6 to 6
Outputs:
- view_grad: bfloat16 [8192, 4096], P('pairs', 'dims')
- pre_grad: bfloat16 [8192, 4096], P('pairs', 'dims')
All inputs are finite; a program needn't handle non-finite values.
Results may differ from a plain program's by a relative error of at most 0.017.
Values may be sent and summed in bfloat16 or wider, within the bound.
A program may use at most 64 MiB of HBM per device.

v0:
```python
import jax
import jax.numpy as jnp
from jax import lax
from jax.sharding import PartitionSpec as P

D = 4096


inv_weight = 25.0
var_weight = 25.0
cov_weight = 1.0
var_eps = 1e-05
loss_share = 32.0


def on_device(first_view, second_view, weight, pre_act):
    values = first_view.astype(jnp.float32)
    local_rows = values.shape[0]
    total = local_rows * lax.axis_size("pairs")
    column_mean = lax.psum(jnp.sum(values, axis=0), "pairs") / total
    centered = values - column_mean
    variance = lax.psum(jnp.sum(centered * centered, axis=0), "pairs") / (total - 1)
    packed = centered.astype(jnp.bfloat16)
    deviation = jnp.sqrt(variance + var_eps)
    contract_cols = (((1,), (1,)), ((), ()))
    term = lax.dot_general(
        packed,
        lax.all_gather(packed, "pairs", axis=0, tiled=True),
        contract_cols,
        preferred_element_type=jnp.float32,
    )
    gram_packed = lax.psum(term.astype(jnp.bfloat16), "dims")
    cov_prod = jnp.dot(
        gram_packed,
        lax.all_gather(packed, "pairs", axis=0, tiled=True),
        preferred_element_type=jnp.float32,
    )
    factor = total * D / loss_share
    invariance = 2.0 * inv_weight / (total * D) * (values - second_view.astype(jnp.float32))
    hinge = jnp.where(deviation < 1.0, 1.0, 0.0).astype(jnp.float32)
    spread_term = -var_weight / D * hinge * centered / ((total - 1) * deviation)
    cov_term = 4.0 * cov_weight / (D * (total - 1)) * (cov_prod / (total - 1) - centered * variance)
    view_grad = (factor * (invariance + spread_term + cov_term)).astype(jnp.bfloat16)
    back = lax.dot_general(view_grad, weight, contract_cols, preferred_element_type=jnp.float32)
    share = lax.psum_scatter(back, "dims", scatter_dimension=1, tiled=True)
    pre_grad = jnp.where(pre_act > 0, share, 0.0).astype(jnp.bfloat16)
    return (view_grad, pre_grad)


def solution(mesh):
    return jax.shard_map(
        on_device,
        mesh=mesh,
        in_specs=(P("pairs", "dims"), P("pairs", "dims"), P(None, "dims"), P("pairs", "dims")),
        out_specs=(P("pairs", "dims"), P("pairs", "dims")),
        check_vma=False,
    )
```

profile of v0, /device:TPU:1, one launch (start us, length us, event | category | flops | bytes accessed | tf_op | source)
XLA Modules:
  0.0 700.3 jit_solution(9935675161194552124)
XLA Ops:
  7.2 0.0 all-gather.2.cloned.1.call-start
  7.2 0.9 convert_reduce_fusion
  8.2 204.4 %psum.21 = f32[512]{0:T(512)S(1)} all-reduce(f32[512]{0:T(512)S(1)} %convert_reduce_fusion), channel_id=1, replica_groups=mesh['pairs'=64,'dims'=8] {'pairs'}, use_global_device_ids=true, to_apply=%region_1.0 | all-reduce | flops 512 | bytes 4096 | tf_op jit(solution)/shard_map/psum | solution.py:20
  212.6 1.6 fusion.9
  214.2 0.0 all-gather.2.cloned.1.call-update
  214.2 0.0 copy-start.1
  214.2 0.0 copy-start.3
  214.2 0.0 all-reduce.2.cloned.1.call-start
  214.3 205.1 %all-gather.2.cloned.1.call-done = bf16[8192,512]{1,0:T(8,128)(2,1)} async-done(((bf16[128,512]{1,0:T(8,128)(2,1)}), bf16[8192,512]{1,0:T(8,128)(2,1)}) %all-gather.2.cloned.1.call-update) | async-done | bytes 8388624 | tf_op jit(solution)/shard_map/all_gather | solution.py:28
  419.4 7.6 %convolution_convert_fusion = bf16[128,8192]{1,0:T(8,128)(2,1)} fusion(bf16[128,512]{1,0:T(8,128)(2,1)} %get-tuple-element.3, bf16[8192,512]{1,0:T(8,128)(2,1)} %all-gather.2.cloned.1.call-done), kind=kOutput, calls=%fused_computation | convolution fusion | flops 1074790400 | bytes 10616832 | tf_op jit(solution)/shard_map/dot_general | solution.py:26
  426.9 0.0 all-reduce.2.cloned.1.call-update
  426.9 0.0 reduce-scatter.2.cloned.1.call-start
  427.0 188.5 %psum.22 = f32[512]{0:T(512)S(1)} all-reduce(f32[512]{0:T(512)S(1)} %get-tuple-element.2), channel_id=1, replica_groups=mesh['pairs'=64,'dims'=8] {'pairs'}, use_global_device_ids=true, to_apply=%region_3.0 | all-reduce | flops 512 | bytes 4096 | tf_op jit(solution)/shard_map/psum | solution.py:22
  615.5 0.0 all-reduce.2.cloned.1.call-done
  615.6 0.0 copy-done.1
  615.6 0.0 copy-done.3
  615.6 0.0 copy-start
  615.6 5.5 fusion.4
  621.1 0.0 copy-done
  621.1 0.0 copy-start.2
  621.1 0.0 copy-start.4
  621.1 2.8 fusion.14
  623.9 0.0 reduce-scatter.2.cloned.1.call-update
  623.9 0.0 copy-done.2
  623.9 68.1 %reduce-scatter.2.cloned.1.call-done = f32[128,512]{1,0:T(8,128)} async-done(((f32[128,4096]{1,0:T(8,128)}), f32[128,512]{1,0:T(8,128)}) %reduce-scatter.2.cloned.1.call-update) | async-done | bytes 262160 | tf_op jit(solution)/shard_map/reduce_scatter | solution.py:45
  692.1 0.0 copy-done.4
  692.1 1.6 select_convert_fusion
  (2 shorter events, 0.0 us)
Async XLA Ops:
  7.2 412.2 %all-gather.2.cloned.1.call-start = ((), (), s32[]{:S(2)}) async-start(), calls=%async_computation.1 | async-start | bytes 8519680 | tf_op jit(solution)/shard_map/all_gather | solution.py:28
  214.2 401.4 %copy-start.1 = (bf16[128,512]{1,0:T(8,128)(2,1)S(1)}, bf16[128,512]{1,0:T(8,128)(2,1)}, u32[]{:S(2)}) copy-start(bf16[128,512]{1,0:T(8,128)(2,1)} %param.4) | copy-start | bytes 393220
  214.2 401.4 %copy-start.3 = (bf16[128,512]{1,0:T(8,128)(2,1)S(1)}, bf16[128,512]{1,0:T(8,128)(2,1)}, u32[]{:S(2)}) copy-start(bf16[128,512]{1,0:T(8,128)(2,1)} %param.5) | copy-start | bytes 393220
  214.2 401.3 %all-reduce.2.cloned.1.call-start = ((), (), s32[]{:S(2)}) async-start(), calls=%async_computation.2 | async-start | bytes 4194304 | tf_op jit(solution)/shard_map/psum | solution.py:32
  426.9 265.1 %reduce-scatter.2.cloned.1.call-start = ((), (), s32[]{:S(2)}) async-start(), calls=%async_computation.3 | async-start | bytes 2359296 | tf_op jit(solution)/shard_map/reduce_scatter | solution.py:45
  615.6 5.5 copy-start
  621.1 2.9 copy-start.2
  621.1 71.0 %copy-start.4 = (bf16[128,512]{1,0:T(8,128)(2,1)S(1)}, bf16[128,512]{1,0:T(8,128)(2,1)}, u32[]{:S(2)}) copy-start(bf16[128,512]{1,0:T(8,128)(2,1)} %param.7) | copy-start | bytes 393220
Sparse Core Ops, SparseCore 0:
  214.3 204.9 all-gather.1
  427.1 80.0 all-reduce.1
  624.1 67.9 reduce-scatter.1
where the time goes:
time: 702 us; the launch traced here: 700 us
  blocking collectives  393 us (56%)
  waiting for transfers between devices  273 us (39%)
  matrix products  15.8 us (2%)
  between operations  13.8 us (2%)
    all_gather x1, waiting for transfers between devices, on_device(): lax.all_gather(packed, 'pairs', axis=0, tiled=True)  205 us
    psum x1, blocking collectives, on_device(): column_mean = lax.psum(jnp.sum(values, axis=0), 'pairs') / total  204 us
    psum x1, blocking collectives, on_device(): lax.psum(jnp.sum(centered * centered, axis=0), 'pairs') / (total - 1)  189 us
    reduce_scatter x1, waiting for transfers between devices, on_device(): share = lax.psum_scatter(back, 'dims', scatter_dimension=1, tiled=True)  68.1 us
  transfers between devices with their start and end apart: 3, of which 2 were waited for; matrix products, arithmetic and copies ran while one was open for 0% of the time, Pallas kernels for 0%

commit v1 on v0

v1 whole, which is shorter than its diff:
```python
import jax
import jax.numpy as jnp
from jax import lax
from jax.experimental import pallas as pl
from jax.experimental.pallas import tpu as pltpu
from jax.sharding import PartitionSpec as P

D = 4096
N = 8192
ROWS = 128
COLS = 512
UNIT = 64

inv_weight = 25.0
var_weight = 25.0
cov_weight = 1.0
var_eps = 1e-05
loss_share = 32.0

F32 = jnp.float32
BF16 = jnp.bfloat16
NT = (((1,), (1,)), ((), ()))
TN = (((0,), (0,)), ((), ()))


def kernel(
    fv, sv, w, pa, vg_out, pg_out,
    xj, xk, pj, pk, svb, wb, pab,
    own, st1, tot, st2, msq, st3,
    cf, rs_s, rs_r, yh_s, yh_r, call,
    cx_s, cx_r, db_s, db_r, bk_s, bk_r, keep,
    lsem,
    xj_ss, xj_rs, xk_ss, xk_rs,
    s1_ss, s1_rs, s2_ss, s2_rs, s3_ss, s3_rs,
    pk_ss, pk_rs, rsz_ss, rsz_rs, yh_ss, yh_rs, ag_ss, ag_rs,
    cx_ss, cx_rs, db_ss, db_rs, bk_ss, bk_rs,
):
    p = lax.axis_index("pairs")
    d = lax.axis_index("dims")
    z, yh, x = p // 8, (p // 4) % 2, p % 4
    yl, c = d // 2, d % 2

    def dev(z_, yh_, x_, yl_, c_):
        return (z_ * 8 + yh_ * 4 + x_, yl_ * 2 + c_)

    def to_x(r):
        return dev(z, yh, (x + r) % 4, yl, c)

    def to_k(r):
        return dev(z, yh, yl, (x + r) % 4, c)

    def from_k(r):
        return dev(z, yh, (yl + 4 - r) % 4, x, c)

    def to_yl(r):
        return dev(z, yh, x, (yl + r) % 4, c)

    def to_zy(r):
        return dev((z + r % 8) % 8, (yh + r // 8) % 2, x, yl, c)

    partner = dev(z, yh, x, yl, 1 - c)
    diagonal = x == yl

    def remote(src, dst, ss, rs, to):
        return pltpu.make_async_remote_copy(
            src_ref=src, dst_ref=dst, send_sem=ss, recv_sem=rs,
            device_id=to, device_id_type=pl.DeviceIdType.MESH)

    load_x = pltpu.make_async_copy(fv, xj.at[x], lsem.at[0])
    load_x.start()
    load_w = pltpu.make_async_copy(w, wb, lsem.at[1])
    load_s = pltpu.make_async_copy(sv, svb, lsem.at[2])
    load_p = pltpu.make_async_copy(pa, pab, lsem.at[3])
    load_k = pltpu.make_async_copy(fv, xk.at[x], lsem.at[4])

    barrier = pltpu.get_barrier_semaphore()

    def greet(to):
        pl.semaphore_signal(barrier, inc=1, device_id=to, device_id_type=pl.DeviceIdType.MESH)

    count = 0
    for r in range(1, 16):
        greet(to_zy(r))
        count += 1
    for r in range(1, 4):
        greet(to_x(r))
        greet(to_k(r))
        greet(from_k(r))
        greet(to_yl(r))
        count += 4
    greet(partner)
    count += 1

    @pl.when(jnp.logical_not(diagonal))
    def _():
        greet(to_k(0))
        greet(from_k(0))

    @pl.when(diagonal)
    def _():
        load_k.start()

    load_w.start()
    load_s.start()
    load_p.start()
    load_x.wait()
    own[...] = jnp.sum(xj[x].astype(F32), axis=0, keepdims=True)

    @pl.when(jnp.logical_not(diagonal))
    def _():
        pl.semaphore_wait(barrier, count + 2)

    @pl.when(diagonal)
    def _():
        pl.semaphore_wait(barrier, count)

    s1j = [remote(own, st1.at[0, r], s1_ss.at[0, r], s1_rs.at[0, r], to_x(r)) for r in range(1, 4)]
    s1k = [remote(own, st1.at[1, r], s1_ss.at[1, r], s1_rs.at[1, r], to_k(r)) for r in range(4)]
    gj = [remote(xj.at[x], xj.at[x], xj_ss.at[r], xj_rs.at[r], to_x(r)) for r in range(1, 4)]
    gk = [remote(xj.at[x], xk.at[x], xk_ss.at[r], xk_rs.at[r], to_k(r)) for r in range(4)]
    for cp in s1j + s1k[1:]:
        cp.start()

    @pl.when(jnp.logical_not(diagonal))
    def _():
        s1k[0].start()
        gk[0].start()

    for cp in gk[1:] + gj:
        cp.start()

    @pl.when(diagonal)
    def _():
        st1[1, 0] = own[...]

    for cp in s1j:
        cp.wait_recv()
    tot[0] = own[...] + st1[0, 1] + st1[0, 2] + st1[0, 3]

    @pl.when(jnp.logical_not(diagonal))
    def _():
        s1k[0].wait_recv()

    for cp in s1k[1:]:
        cp.wait_recv()
    tot[1] = st1[1, 0] + st1[1, 1] + st1[1, 2] + st1[1, 3]
    s2 = [remote(tot, st2.at[r], s2_ss.at[r], s2_rs.at[r], to_zy(r)) for r in range(1, 16)]
    for cp in s2:
        cp.start()
    for cp in s2:
        cp.wait_recv()
    mean = tot[...]
    for r in range(1, 16):
        mean = mean + st2[r]
    mean = mean / N
    mean_j, mean_k = mean[0], mean[1]

    for cp in gk[1:]:
        cp.wait_recv()

    @pl.when(jnp.logical_not(diagonal))
    def _():
        gk[0].wait_recv()

    @pl.when(diagonal)
    def _():
        load_k.wait()

    @pl.loop(0, 4)
    def _(b):
        pk[0, b] = (xk[b].astype(F32) - mean_k).astype(BF16)

    share = remote(pk.at[0], pk.at[1], pk_ss, pk_rs, partner)
    share.start()
    for cp in gj:
        cp.wait_recv()
    msq[...] = jnp.zeros_like(msq)

    @pl.loop(0, 4)
    def _(b):
        centered = xj[b].astype(F32) - mean_j
        pj[b] = centered.astype(BF16)
        msq[...] += jnp.sum(centered * centered, axis=0, keepdims=True)

    s3 = [remote(msq, st3.at[r], s3_ss.at[r], s3_rs.at[r], to_zy(r)) for r in range(1, 16)]

    def block(h):
        prod = lax.dot_general(
            pj[...].reshape(4 * ROWS, COLS), pk[h].reshape(4 * ROWS, COLS), TN,
            preferred_element_type=F32)
        cf[h] = prod.reshape(8, UNIT, COLS)

    block(0)
    share.wait_recv()
    block(1)

    def near(way):
        return dev((z + (1 if way == 0 else 7)) % 8, yh, x, yl, c)

    rs = {}
    for n in range(7):
        for way in range(2):
            h = (n + way) % 2
            k = 4 - (n + 1) // 2
            unit = (z + (k if way == 0 else 8 - k)) % 8
            val = cf[h, unit]
            if n >= 2:
                rs[n - 2, way].wait_recv()
                val = val + rs_r[way, n - 2].astype(F32)
            rs_s[way, n] = val.astype(BF16)
            rs[n, way] = remote(
                rs_s.at[way, n], rs_r.at[way, n], rsz_ss.at[way, n], rsz_rs.at[way, n], near(way))
            rs[n, way].start()
        if n == 1:
            for cp in s3:
                cp.start()
    swap = []
    for n in (5, 6):
        rs[n, 0].wait_recv()
        rs[n, 1].wait_recv()
    for h in range(2):
        mine = cf[h, z] + rs_r[0, 6 - h].astype(F32) + rs_r[1, 5 + h].astype(F32)
        cf[h, z] = mine
        yh_s[h] = mine.astype(BF16)
        cp = remote(yh_s.at[h], yh_r.at[h], yh_ss.at[h], yh_rs.at[h], to_zy(8))
        cp.start()
        swap.append(cp)
    for h in range(2):
        swap[h].wait_recv()
        call[h, z] = (cf[h, z] + yh_r[h].astype(F32)).astype(BF16)

    ag = {}
    for n in range(7):
        for way in range(2):
            h = (n + way) % 2
            o = n // 2
            unit = (z + (8 - o if way == 0 else o)) % 8
            if n >= 2:
                ag[n - 2, way].wait_recv()
            ag[n, way] = remote(
                call.at[h, unit], call.at[h, unit], ag_ss.at[way, n], ag_rs.at[way, n], near(way))
            ag[n, way].start()

    for cp in s3:
        cp.wait_recv()
    variance = msq[...]
    for r in range(1, 16):
        variance = variance + st3[r]
    variance = variance / (N - 1)
    deviation = jnp.sqrt(variance + var_eps)
    hinge = jnp.where(deviation < 1.0, 1.0, 0.0).astype(F32)
    for n in (5, 6):
        ag[n, 0].wait_recv()
        ag[n, 1].wait_recv()

    def product(b):
        out = lax.dot_general(
            pk[0, b], call[0].reshape(8 * UNIT, COLS), NT, preferred_element_type=F32)
        return out + lax.dot_general(
            pk[1, b], call[1].reshape(8 * UNIT, COLS), NT, preferred_element_type=F32)

    cx = []
    for r in (2, 1, 3):
        cx_s[r] = product((x + r) % 4).astype(BF16)
        cp = remote(cx_s.at[r], cx_r.at[r], cx_ss.at[r], cx_rs.at[r], to_x(r))
        cp.start()
        cx.append(cp)
    cov_prod = product(x)
    load_s.wait()
    for cp in cx:
        cp.wait_recv()
    for r in range(1, 4):
        cov_prod = cov_prod + cx_r[r].astype(F32)

    values = xj[x].astype(F32)
    centered = values - mean_j
    factor = N * D / loss_share
    invariance = 2.0 * inv_weight / (N * D) * (values - svb[...].astype(F32))
    spread_term = -var_weight / D * hinge * centered / ((N - 1) * deviation)
    cov_term = 4.0 * cov_weight / (D * (N - 1)) * (cov_prod / (N - 1) - centered * variance)
    vg = (factor * (invariance + spread_term + cov_term)).astype(BF16)
    vg_out[...] = vg

    load_w.wait()
    load_p.wait()

    def back(r, core):
        at = pl.multiple_of((((yl + r) % 4) * 2 + core) * COLS, COLS)
        return lax.dot_general(
            vg_out[...], wb[pl.ds(at, COLS), :], NT, preferred_element_type=F32)

    db = {}
    for r in (2, 1, 3, 0):
        db_s[r] = back(r, 1 - c).astype(BF16)
        db[r] = remote(db_s.at[r], db_r.at[r], db_ss.at[r], db_rs.at[r], partner)
        db[r].start()
    bk = []
    for r in (2, 1, 3, 0):
        mine = back(r, c)
        db[r].wait_recv()
        mine = mine + db_r[r].astype(F32)
        if r == 0:
            keep[...] = mine
        else:
            bk_s[r] = mine.astype(BF16)
            cp = remote(bk_s.at[r], bk_r.at[r], bk_ss.at[r], bk_rs.at[r], to_yl(r))
            cp.start()
            bk.append(cp)
    for cp in bk:
        cp.wait_recv()
    total = keep[...]
    for r in range(1, 4):
        total = total + bk_r[r].astype(F32)
    pg_out[...] = jnp.where(pab[...] > 0, total, 0.0).astype(BF16)

    for cp in s1j + s1k[1:] + gj + gk[1:] + s2 + s3 + [share] + swap + cx + bk:
        cp.wait_send()
    for group in (rs, ag, db):
        for cp in group.values():
            cp.wait_send()

    @pl.when(jnp.logical_not(diagonal))
    def _():
        s1k[0].wait_send()
        gk[0].wait_send()


def on_device(first_view, second_view, weight, pre_act):
    dma = pltpu.SemaphoreType.DMA
    vmem = pltpu.VMEM
    return pl.pallas_call(
        kernel,
        out_shape=[jax.ShapeDtypeStruct((ROWS, COLS), BF16)] * 2,
        in_specs=[pl.BlockSpec(memory_space=pl.ANY)] * 4,
        out_specs=[pl.BlockSpec(memory_space=pltpu.VMEM)] * 2,
        scratch_shapes=[
            vmem((4, ROWS, COLS), BF16),
            vmem((4, ROWS, COLS), BF16),
            vmem((4, ROWS, COLS), BF16),
            vmem((2, 4, ROWS, COLS), BF16),
            vmem((ROWS, COLS), BF16),
            vmem((D, COLS), BF16),
            vmem((ROWS, COLS), BF16),
            vmem((1, COLS), F32),
            vmem((2, 4, 1, COLS), F32),
            vmem((2, 1, COLS), F32),
            vmem((16, 2, 1, COLS), F32),
            vmem((1, COLS), F32),
            vmem((16, 1, COLS), F32),
            vmem((2, 8, UNIT, COLS), F32),
            vmem((2, 7, UNIT, COLS), BF16),
            vmem((2, 7, UNIT, COLS), BF16),
            vmem((2, UNIT, COLS), BF16),
            vmem((2, UNIT, COLS), BF16),
            vmem((2, 8, UNIT, COLS), BF16),
            vmem((4, ROWS, COLS), BF16),
            vmem((4, ROWS, COLS), BF16),
            vmem((4, ROWS, COLS), BF16),
            vmem((4, ROWS, COLS), BF16),
            vmem((4, ROWS, COLS), BF16),
            vmem((4, ROWS, COLS), BF16),
            vmem((ROWS, COLS), F32),
            dma((5,)),
            dma((4,)), dma((4,)), dma((4,)), dma((4,)),
            dma((2, 4)), dma((2, 4)), dma((16,)), dma((16,)), dma((16,)), dma((16,)),
            dma, dma, dma((2, 7)), dma((2, 7)), dma((2,)), dma((2,)), dma((2, 7)), dma((2, 7)),
            dma((4,)), dma((4,)), dma((4,)), dma((4,)), dma((4,)), dma((4,)),
        ],
        compiler_params=pltpu.CompilerParams(
            collective_id=0, has_side_effects=True, vmem_limit_bytes=48 * 2**20),
        cost_estimate=pl.CostEstimate(flops=2700000000, bytes_accessed=5000000, transcendentals=0),
        name="vicreg_backward",
    )(first_view, second_view, weight, pre_act)


def solution(mesh):
    return jax.shard_map(
        on_device,
        mesh=mesh,
        in_specs=(P("pairs", "dims"), P("pairs", "dims"), P(None, "dims"), P("pairs", "dims")),
        out_specs=(P("pairs", "dims"), P("pairs", "dims")),
        check_vma=False,
    )
```

time: 702 us -> 102 us (0.15)
  blocking collectives: 393 us -> 0 us
  waiting for transfers between devices: 273 us -> 0 us
  Pallas kernels: 0 us -> 94 us
  matrix products: 15.8 us -> 0 us
  between operations: 13.8 us -> 0.65 us
    psum x2 -> x0, blocking collectives: 393 us -> none  [the longest x1 204 us: on_device(): column_mean = lax.psum(jnp.sum(values, axis=0), 'pairs') / total]
    all_gather x1 -> x0, waiting for transfers between devices: 205 us -> none  [on_device(): lax.all_gather(packed, 'pairs', axis=0, tiled=True)]
    pallas_call x0 -> x1, Pallas kernels: none -> 94 us  [on_device(): pl.pallas_call(kernel, out_shape=[jax.ShapeDtypeStruct((ROWS, COLS), BF16...]
    reduce_scatter x1 -> x0, waiting for transfers between devices: 68.1 us -> none  [on_device(): share = lax.psum_scatter(back, 'dims', scatter_dimension=1, tiled=True)]
    dot_general x3 -> x0, matrix products: 15.8 us -> none  [the longest x1 7.57 us: on_device(): lax.dot_general(packed, lax.all_gather(packed, 'pairs', axis=0, tiled=Tru...]
  transfers between devices with their start and end apart: 3 -> 0, of which waited for: 2 -> 0; matrix products, arithmetic and copies ran while one was open for 0% -> 0% of each run, Pallas kernels for 0% -> 0%
where the time goes in v1:
time: 102 us; the launch traced here: 101 us
  Pallas kernels  94 us (92%)
  local copies, waits for them, and re-layouts  6.2 us (6%)
    pallas_call x1, Pallas kernels, on_device(): pl.pallas_call(kernel, out_shape=[jax.ShapeDtypeStruct((ROWS, COLS), BF16...  94 us
    unnamed x10, local copies, waits for them, and re-layouts  6.2 us

profile of v1, /device:TPU:1, one launch (start us, length us, event | category | flops | bytes accessed | tf_op | source)
XLA Modules:
  0.0 100.8 jit_solution(11237392915890004317)
XLA Ops:
  0.6 0.0 copy-start
  0.6 2.2 %copy-done = bf16[4096,512]{1,0:T(8,128)(2,1)S(1)} copy-done((bf16[4096,512]{1,0:T(8,128)(2,1)S(1)}, bf16[4096,512]{1,0:T(8,128)(2,1)}, u32[]{:S(2)}) %copy-start) | copy-done | bytes 4194328
  2.8 0.0 copy-start.1
  2.8 0.9 copy-done.1
  3.7 0.0 copy-start.2
  3.7 0.9 copy-done.2
  4.6 0.0 copy-start.3
  4.6 0.9 copy-done.3
  5.5 94.0 %vicreg_backward.1 = (bf16[128,512]{1,0:T(8,128)(2,1)S(1)}, bf16[128,512]{1,0:T(8,128)(2,1)S(1)}) custom-call(bf16[128,512]{1,0:T(8,128)(2,1)S(1)} %copy-done.1, bf16[128,512]{1,0:T(8,128)(2,1)S(1)} %copy-done.2, bf16[4096,512]{1,0:T(8,128)(2,1)S(1)} %copy-done, bf16[128,512]{1,0:T(8,128)(2,1)S(1)} %copy-done.3), custom_call_target="tpu_custom_call" | custom-call | flops 2700000000 | bytes 5000000 | tf_op jit(solution)/shard_map/vicreg_backward/pallas_call | solution.py:331
  99.5 0.7 copy.8
  100.2 0.7 copy.9
Async XLA Ops:
  0.6 2.2 %copy-start = (bf16[4096,512]{1,0:T(8,128)(2,1)S(1)}, bf16[4096,512]{1,0:T(8,128)(2,1)}, u32[]{:S(2)}) copy-start(bf16[4096,512]{1,0:T(8,128)(2,1)} %w.1) | copy-start | bytes 12582916
  2.8 0.9 copy-start.1
  3.7 0.9 copy-start.2
  4.6 0.9 copy-start.3

commit v2 on v1

--- a/solution.py
+++ b/solution.py
@@ -9,7 +9,7 @@
 N = 8192
 ROWS = 128
 COLS = 512
-UNIT = 64
+UNIT = 32
 
 inv_weight = 25.0
 var_weight = 25.0
@@ -28,7 +28,7 @@
     xj, xk, pj, pk, svb, wb, pab,
     own, st1, tot, st2, msq, st3,
     cf, rs_s, rs_r, yh_s, yh_r, call,
-    cx_s, cx_r, db_s, db_r, bk_s, bk_r, keep,
+    cov, cx_s, cx_r, db_s, db_r, bk_s, bk_r, keep,
     lsem,
     xj_ss, xj_rs, xk_ss, xk_rs,
     s1_ss, s1_rs, s2_ss, s2_rs, s3_ss, s3_rs,
@@ -188,58 +188,86 @@
         prod = lax.dot_general(
             pj[...].reshape(4 * ROWS, COLS), pk[h].reshape(4 * ROWS, COLS), TN,
             preferred_element_type=F32)
-        cf[h] = prod.reshape(8, UNIT, COLS)
+        cf[h] = prod.reshape(2, 8, UNIT, COLS)
+
+    def along(way, hops):
+        return dev((z + (hops if way == 0 else 8 - hops)) % 8, yh, x, yl, c)
+
+    def unit(way, hops):
+        return (z + (hops if way == 0 else 8 - hops)) % 8
+
+    sent = []
+    rs = {}
+
+    def reduce_step(q, h, way, k):
+        if k == 4 and h != way:
+            return
+        val = cf[h, q, unit(way, k)]
+        for m in {2: (4, 3), 1: (2,)}.get(k, ()):
+            if (q, h, way, m) in rs:
+                rs[q, h, way, m].wait_recv()
+                val = val + rs_r[q, h, way, m - 1].astype(F32)
+        at = (q, h, way, k - 1)
+        rs_s[at] = val.astype(BF16)
+        cp = remote(rs_s.at[at], rs_r.at[at], rsz_ss.at[at], rsz_rs.at[at],
+                    along(way, 2 if k == 4 else 1))
+        cp.start()
+        rs[q, h, way, k] = cp
+        sent.append(cp)
 
     block(0)
+    for q in range(2):
+        for way in range(2):
+            reduce_step(q, 0, way, 4)
+            reduce_step(q, 0, way, 3)
     share.wait_recv()
     block(1)
-
-    def near(way):
-        return dev((z + (1 if way == 0 else 7)) % 8, yh, x, yl, c)
-
-    rs = {}
-    for n in range(7):
+    for q in range(2):
         for way in range(2):
-            h = (n + way) % 2
-            k = 4 - (n + 1) // 2
-            unit = (z + (k if way == 0 else 8 - k)) % 8
-            val = cf[h, unit]
-            if n >= 2:
-                rs[n - 2, way].wait_recv()
-                val = val + rs_r[way, n - 2].astype(F32)
-            rs_s[way, n] = val.astype(BF16)
-            rs[n, way] = remote(
-                rs_s.at[way, n], rs_r.at[way, n], rsz_ss.at[way, n], rsz_rs.at[way, n], near(way))
-            rs[n, way].start()
-        if n == 1:
-            for cp in s3:
-                cp.start()
-    swap = []
-    for n in (5, 6):
-        rs[n, 0].wait_recv()
-        rs[n, 1].wait_recv()
-    for h in range(2):
-        mine = cf[h, z] + rs_r[0, 6 - h].astype(F32) + rs_r[1, 5 + h].astype(F32)
-        cf[h, z] = mine
-        yh_s[h] = mine.astype(BF16)
-        cp = remote(yh_s.at[h], yh_r.at[h], yh_ss.at[h], yh_rs.at[h], to_zy(8))
-        cp.start()
-        swap.append(cp)
-    for h in range(2):
-        swap[h].wait_recv()
-        call[h, z] = (cf[h, z] + yh_r[h].astype(F32)).astype(BF16)
+            reduce_step(q, 1, way, 4)
+            reduce_step(q, 1, way, 3)
+    for cp in s3:
+        cp.start()
+    for k in (2, 1):
+        for q in range(2):
+            for h in range(2):
+                for way in range(2):
+                    reduce_step(q, h, way, k)
+
+    swap = {}
+    for q in range(2):
+        for h in range(2):
+            mine = cf[h, q, z]
+            for way in range(2):
+                rs[q, h, way, 1].wait_recv()
+                mine = mine + rs_r[q, h, way, 0].astype(F32)
+            cf[h, q, z] = mine
+            yh_s[q, h] = mine.astype(BF16)
+            cp = remote(yh_s.at[q, h], yh_r.at[q, h], yh_ss.at[q, h], yh_rs.at[q, h], to_zy(8))
+            cp.start()
+            swap[q, h] = cp
+            sent.append(cp)
 
     ag = {}
-    for n in range(7):
-        for way in range(2):
-            h = (n + way) % 2
-            o = n // 2
-            unit = (z + (8 - o if way == 0 else o)) % 8
-            if n >= 2:
-                ag[n - 2, way].wait_recv()
-            ag[n, way] = remote(
-                call.at[h, unit], call.at[h, unit], ag_ss.at[way, n], ag_rs.at[way, n], near(way))
-            ag[n, way].start()
+
+    def gather_step(q, h, way, k):
+        if k == 4 and h != way:
+            return
+        if k > 1 and k != 4:
+            ag[q, h, way, k - 1].wait_recv()
+        at = (q, h, way, k - 1)
+        held = call.at[h, q, unit(1 - way, min(k, 3) - 1)]
+        cp = remote(held, held, ag_ss.at[at], ag_rs.at[at], along(way, 2 if k == 4 else 1))
+        cp.start()
+        ag[q, h, way, k] = cp
+        sent.append(cp)
+
+    for q in range(2):
+        for h in range(2):
+            swap[q, h].wait_recv()
+            call[h, q, z] = (cf[h, q, z] + yh_r[q, h].astype(F32)).astype(BF16)
+            for way in range(2):
+                gather_step(q, h, way, 1)
 
     for cp in s3:
         cp.wait_recv()
@@ -249,37 +277,52 @@
     variance = variance / (N - 1)
     deviation = jnp.sqrt(variance + var_eps)
     hinge = jnp.where(deviation < 1.0, 1.0, 0.0).astype(F32)
-    for n in (5, 6):
-        ag[n, 0].wait_recv()
-        ag[n, 1].wait_recv()
-
-    def product(b):
+    for k in (2, 3):
+        for q in range(2):
+            for h in range(2):
+                for way in range(2):
+                    gather_step(q, h, way, k)
+                    if k == 3:
+                        gather_step(q, h, way, 4)
+
+    cx = {}
+
+    def product(q):
+        for h in range(2):
+            for way in range(2):
+                ag[q, h, way, 3].wait_recv()
+                if h == way:
+                    ag[q, h, way, 4].wait_recv()
         out = lax.dot_general(
-            pk[0, b], call[0].reshape(8 * UNIT, COLS), NT, preferred_element_type=F32)
-        return out + lax.dot_general(
-            pk[1, b], call[1].reshape(8 * UNIT, COLS), NT, preferred_element_type=F32)
-
-    cx = []
-    for r in (2, 1, 3):
-        cx_s[r] = product((x + r) % 4).astype(BF16)
-        cp = remote(cx_s.at[r], cx_r.at[r], cx_ss.at[r], cx_rs.at[r], to_x(r))
-        cp.start()
-        cx.append(cp)
-    cov_prod = product(x)
+            pk[0].reshape(4 * ROWS, COLS), call[0, q].reshape(COLS // 2, COLS), NT,
+            preferred_element_type=F32)
+        out = out + lax.dot_general(
+            pk[1].reshape(4 * ROWS, COLS), call[1, q].reshape(COLS // 2, COLS), NT,
+            preferred_element_type=F32)
+        cov[q] = out.reshape(4, ROWS, COLS // 2)
+        for r in (2, 1, 3):
+            cx_s[q, r] = cov[q, (x + r) % 4].astype(BF16)
+            cp = remote(cx_s.at[q, r], cx_r.at[q, r], cx_ss.at[q, r], cx_rs.at[q, r], to_x(r))
+            cp.start()
+            cx[q, r] = cp
+            sent.append(cp)
+
+    product(0)
+    product(1)
     load_s.wait()
-    for cp in cx:
-        cp.wait_recv()
-    for r in range(1, 4):
-        cov_prod = cov_prod + cx_r[r].astype(F32)
-
-    values = xj[x].astype(F32)
-    centered = values - mean_j
     factor = N * D / loss_share
-    invariance = 2.0 * inv_weight / (N * D) * (values - svb[...].astype(F32))
-    spread_term = -var_weight / D * hinge * centered / ((N - 1) * deviation)
-    cov_term = 4.0 * cov_weight / (D * (N - 1)) * (cov_prod / (N - 1) - centered * variance)
-    vg = (factor * (invariance + spread_term + cov_term)).astype(BF16)
-    vg_out[...] = vg
+    for q in range(2):
+        at = slice(q * COLS // 2, (q + 1) * COLS // 2)
+        cov_prod = cov[q, x]
+        for r in range(1, 4):
+            cx[q, r].wait_recv()
+            cov_prod = cov_prod + cx_r[q, r].astype(F32)
+        values = xj[x, :, at].astype(F32)
+        centered = values - mean_j[:, at]
+        invariance = 2.0 * inv_weight / (N * D) * (values - svb[:, at].astype(F32))
+        spread_term = -var_weight / D * hinge[:, at] * centered / ((N - 1) * deviation[:, at])
+        cov_term = 4.0 * cov_weight / (D * (N - 1)) * (cov_prod / (N - 1) - centered * variance[:, at])
+        vg_out[:, at] = (factor * (invariance + spread_term + cov_term)).astype(BF16)
 
     load_w.wait()
     load_p.wait()
@@ -290,12 +333,15 @@
             vg_out[...], wb[pl.ds(at, COLS), :], NT, preferred_element_type=F32)
 
     db = {}
-    for r in (2, 1, 3, 0):
+    bk = []
+
+    def lend(r):
         db_s[r] = back(r, 1 - c).astype(BF16)
         db[r] = remote(db_s.at[r], db_r.at[r], db_ss.at[r], db_rs.at[r], partner)
         db[r].start()
-    bk = []
-    for r in (2, 1, 3, 0):
+        sent.append(db[r])
+
+    def send_back(r):
         mine = back(r, c)
         db[r].wait_recv()
         mine = mine + db_r[r].astype(F32)
@@ -306,6 +352,16 @@
             cp = remote(bk_s.at[r], bk_r.at[r], bk_ss.at[r], bk_rs.at[r], to_yl(r))
             cp.start()
             bk.append(cp)
+            sent.append(cp)
+
+    lend(2)
+    lend(1)
+    send_back(2)
+    lend(3)
+    send_back(1)
+    lend(0)
+    send_back(3)
+    send_back(0)
     for cp in bk:
         cp.wait_recv()
     total = keep[...]
@@ -313,11 +369,8 @@
         total = total + bk_r[r].astype(F32)
     pg_out[...] = jnp.where(pab[...] > 0, total, 0.0).astype(BF16)
 
-    for cp in s1j + s1k[1:] + gj + gk[1:] + s2 + s3 + [share] + swap + cx + bk:
+    for cp in s1j + s1k[1:] + gj + gk[1:] + s2 + s3 + [share] + sent:
         cp.wait_send()
-    for group in (rs, ag, db):
-        for cp in group.values():
-            cp.wait_send()
 
     @pl.when(jnp.logical_not(diagonal))
     def _():
@@ -331,7 +384,7 @@
     return pl.pallas_call(
         kernel,
         out_shape=[jax.ShapeDtypeStruct((ROWS, COLS), BF16)] * 2,
-        in_specs=[pl.BlockSpec(memory_space=pl.ANY)] * 4,
+        in_specs=[pl.BlockSpec(memory_space=pltpu.HBM)] * 4,
         out_specs=[pl.BlockSpec(memory_space=pltpu.VMEM)] * 2,
         scratch_shapes=[
             vmem((4, ROWS, COLS), BF16),
@@ -347,14 +400,15 @@
             vmem((16, 2, 1, COLS), F32),
             vmem((1, COLS), F32),
             vmem((16, 1, COLS), F32),
-            vmem((2, 8, UNIT, COLS), F32),
-            vmem((2, 7, UNIT, COLS), BF16),
-            vmem((2, 7, UNIT, COLS), BF16),
-            vmem((2, UNIT, COLS), BF16),
-            vmem((2, UNIT, COLS), BF16),
-            vmem((2, 8, UNIT, COLS), BF16),
-            vmem((4, ROWS, COLS), BF16),
-            vmem((4, ROWS, COLS), BF16),
+            vmem((2, 2, 8, UNIT, COLS), F32),
+            vmem((2, 2, 2, 4, UNIT, COLS), BF16),
+            vmem((2, 2, 2, 4, UNIT, COLS), BF16),
+            vmem((2, 2, UNIT, COLS), BF16),
+            vmem((2, 2, UNIT, COLS), BF16),
+            vmem((2, 2, 8, UNIT, COLS), BF16),
+            vmem((2, 4, ROWS, COLS // 2), F32),
+            vmem((2, 4, ROWS, COLS // 2), BF16),
+            vmem((2, 4, ROWS, COLS // 2), BF16),
             vmem((4, ROWS, COLS), BF16),
             vmem((4, ROWS, COLS), BF16),
             vmem((4, ROWS, COLS), BF16),
@@ -363,11 +417,12 @@
             dma((5,)),
             dma((4,)), dma((4,)), dma((4,)), dma((4,)),
             dma((2, 4)), dma((2, 4)), dma((16,)), dma((16,)), dma((16,)), dma((16,)),
-            dma, dma, dma((2, 7)), dma((2, 7)), dma((2,)), dma((2,)), dma((2, 7)), dma((2, 7)),
-            dma((4,)), dma((4,)), dma((4,)), dma((4,)), dma((4,)), dma((4,)),
+            dma, dma, dma((2, 2, 2, 4)), dma((2, 2, 2, 4)), dma((2, 2)), dma((2, 2)),
+            dma((2, 2, 2, 4)), dma((2, 2, 2, 4)),
+            dma((2, 4)), dma((2, 4)), dma((4,)), dma((4,)), dma((4,)), dma((4,)),
         ],
         compiler_params=pltpu.CompilerParams(
-            collective_id=0, has_side_effects=True, vmem_limit_bytes=48 * 2**20),
+            collective_id=0, has_side_effects=True, vmem_limit_bytes=60 * 2**20),
         cost_estimate=pl.CostEstimate(flops=2700000000, bytes_accessed=5000000, transcendentals=0),
         name="vicreg_backward",
     )(first_view, second_view, weight, pre_act)

time: 102 us -> 92.8 us (0.910)
  the two profiles are of different devices: /device:TPU:1 before, /device:TPU:17 now
where the time goes in v2:
time: 92.8 us; the launch traced here: 92.6 us
  Pallas kernels  88.9 us (96%)
  local copies, waits for them, and re-layouts  3.14 us (3%)
    pallas_call x1, Pallas kernels, on_device(): pl.pallas_call(kernel, out_shape=[jax.ShapeDtypeStruct((ROWS, COLS), BF16...  88.9 us
    unnamed x2, local copies, waits for them, and re-layouts  3.14 us

profile of v2, /device:TPU:17, one launch (start us, length us, event | category | flops | bytes accessed | tf_op | source)
XLA Modules:
  0.0 92.6 jit_solution(13504010647110054359)
XLA Ops:
  0.6 88.9 %vicreg_backward.1 = (bf16[128,512]{1,0:T(8,128)(2,1)}, bf16[128,512]{1,0:T(8,128)(2,1)}) custom-call(bf16[128,512]{1,0:T(8,128)(2,1)} %fv.1, bf16[128,512]{1,0:T(8,128)(2,1)} %sv.1, bf16[4096,512]{1,0:T(8,128)(2,1)} %w.1, bf16[128,512]{1,0:T(8,128)(2,1)} %pa.1), custom_call_target="tpu_custom_call" | custom-call | flops 2700000000 | bytes 5000000 | tf_op jit(solution)/shard_map/vicreg_backward/pallas_call | solution.py:384
  89.5 1.6 %copy.8 = bf16[128,512]{1,0:T(8,128)(2,1)} copy(bf16[128,512]{1,0:T(8,128)(2,1)} %get-tuple-element.4) | data formatting | bytes 262144
  91.1 1.6 %copy.9 = bf16[128,512]{1,0:T(8,128)(2,1)} copy(bf16[128,512]{1,0:T(8,128)(2,1)} %get-tuple-element.5) | data formatting | bytes 262144

commit v3 on v2

--- a/solution.py
+++ b/solution.py
@@ -8,6 +8,7 @@
 D = 4096
 N = 8192
 ROWS = 128
+HALF = 64
 COLS = 512
 UNIT = 32
 
@@ -28,12 +29,12 @@
     xj, xk, pj, pk, svb, wb, pab,
     own, st1, tot, st2, msq, st3,
     cf, rs_s, rs_r, yh_s, yh_r, call,
-    cov, cx_s, cx_r, db_s, db_r, bk_s, bk_r, keep,
+    cov, cx_s, cx_r, vgp, bk_s, bk_r, keep,
     lsem,
     xj_ss, xj_rs, xk_ss, xk_rs,
     s1_ss, s1_rs, s2_ss, s2_rs, s3_ss, s3_rs,
     pk_ss, pk_rs, rsz_ss, rsz_rs, yh_ss, yh_rs, ag_ss, ag_rs,
-    cx_ss, cx_rs, db_ss, db_rs, bk_ss, bk_rs,
+    cx_ss, cx_rs, vg_ss, vg_rs, bk_ss, bk_rs, w_sem, w_ss, w_rs,
 ):
     p = lax.axis_index("pairs")
     d = lax.axis_index("dims")
@@ -68,7 +69,8 @@
 
     load_x = pltpu.make_async_copy(fv, xj.at[x], lsem.at[0])
     load_x.start()
-    load_w = pltpu.make_async_copy(w, wb, lsem.at[1])
+    load_w = [
+        pltpu.make_async_copy(w.at[i * 2 + c], wb.at[i, 0], w_sem.at[i]) for i in range(4)]
     load_s = pltpu.make_async_copy(sv, svb, lsem.at[2])
     load_p = pltpu.make_async_copy(pa, pab, lsem.at[3])
     load_k = pltpu.make_async_copy(fv, xk.at[x], lsem.at[4])
@@ -100,7 +102,8 @@
     def _():
         load_k.start()
 
-    load_w.start()
+    for cp in load_w:
+        cp.start()
     load_s.start()
     load_p.start()
     load_x.wait()
@@ -127,6 +130,11 @@
         gk[0].start()
 
     for cp in gk[1:] + gj:
+        cp.start()
+
+    lend_w = [
+        remote(w.at[i * 2 + 1 - c], wb.at[i, 1], w_ss.at[i], w_rs.at[i], partner) for i in range(4)]
+    for cp in lend_w:
         cp.start()
 
     @pl.when(diagonal)
@@ -286,6 +294,7 @@
                         gather_step(q, h, way, 4)
 
     cx = {}
+    halves = (slice(0, HALF), slice(HALF, ROWS))
 
     def product(q):
         for h in range(2):
@@ -300,68 +309,73 @@
             pk[1].reshape(4 * ROWS, COLS), call[1, q].reshape(COLS // 2, COLS), NT,
             preferred_element_type=F32)
         cov[q] = out.reshape(4, ROWS, COLS // 2)
-        for r in (2, 1, 3):
-            cx_s[q, r] = cov[q, (x + r) % 4].astype(BF16)
-            cp = remote(cx_s.at[q, r], cx_r.at[q, r], cx_ss.at[q, r], cx_rs.at[q, r], to_x(r))
-            cp.start()
-            cx[q, r] = cp
-            sent.append(cp)
+        for rows in ((slice(0, ROWS),) if q == 0 else halves):
+            part = rows.start // HALF
+            for r in (2, 1, 3):
+                cx_s[q, r, rows] = cov[q, (x + r) % 4, rows].astype(BF16)
+                cp = remote(cx_s.at[q, r, rows], cx_r.at[q, r, rows], cx_ss.at[q, r, part],
+                            cx_rs.at[q, r, part], to_x(r))
+                cp.start()
+                cx[q, r, part] = cp
+                sent.append(cp)
 
     product(0)
     product(1)
     load_s.wait()
     factor = N * D / loss_share
-    for q in range(2):
+    vgc = {}
+
+    def view_grad(q, part):
         at = slice(q * COLS // 2, (q + 1) * COLS // 2)
-        cov_prod = cov[q, x]
+        rows = halves[part]
+        cov_prod = cov[q, x, rows]
         for r in range(1, 4):
-            cx[q, r].wait_recv()
-            cov_prod = cov_prod + cx_r[q, r].astype(F32)
-        values = xj[x, :, at].astype(F32)
+            if (q, r, part) in cx:
+                cx[q, r, part].wait_recv()
+            cov_prod = cov_prod + cx_r[q, r, rows].astype(F32)
+        values = xj[x, rows, at].astype(F32)
         centered = values - mean_j[:, at]
-        invariance = 2.0 * inv_weight / (N * D) * (values - svb[:, at].astype(F32))
+        invariance = 2.0 * inv_weight / (N * D) * (values - svb[rows, at].astype(F32))
         spread_term = -var_weight / D * hinge[:, at] * centered / ((N - 1) * deviation[:, at])
         cov_term = 4.0 * cov_weight / (D * (N - 1)) * (cov_prod / (N - 1) - centered * variance[:, at])
-        vg_out[:, at] = (factor * (invariance + spread_term + cov_term)).astype(BF16)
-
-    load_w.wait()
-    load_p.wait()
-
-    def back(r, core):
-        at = pl.multiple_of((((yl + r) % 4) * 2 + core) * COLS, COLS)
-        return lax.dot_general(
-            vg_out[...], wb[pl.ds(at, COLS), :], NT, preferred_element_type=F32)
-
-    db = {}
+        vg_out[rows, at] = (factor * (invariance + spread_term + cov_term)).astype(BF16)
+        cp = remote(vg_out.at[rows, at], vgp.at[rows, at], vg_ss.at[q, part], vg_rs.at[q, part], partner)
+        cp.start()
+        vgc[q, part] = cp
+        sent.append(cp)
+
     bk = []
 
-    def lend(r):
-        db_s[r] = back(r, 1 - c).astype(BF16)
-        db[r] = remote(db_s.at[r], db_r.at[r], db_ss.at[r], db_rs.at[r], partner)
-        db[r].start()
-        sent.append(db[r])
-
-    def send_back(r):
-        mine = back(r, c)
-        db[r].wait_recv()
-        mine = mine + db_r[r].astype(F32)
-        if r == 0:
-            keep[...] = mine
-        else:
-            bk_s[r] = mine.astype(BF16)
-            cp = remote(bk_s.at[r], bk_r.at[r], bk_ss.at[r], bk_rs.at[r], to_yl(r))
+    def back(part, r):
+        rows = halves[part]
+        at = (yl + r) % 4
+        out = lax.dot_general(vg_out[rows], wb[at, 0], NT, preferred_element_type=F32)
+        return out + lax.dot_general(vgp[rows], wb[at, 1], NT, preferred_element_type=F32)
+
+    def send_back(part):
+        rows = halves[part]
+        for q in range(2):
+            vgc[q, part].wait_recv()
+        for r in (2, 1, 3):
+            bk_s[r, rows] = back(part, r).astype(BF16)
+            cp = remote(bk_s.at[r, rows], bk_r.at[r, rows], bk_ss.at[r, part], bk_rs.at[r, part], to_yl(r))
             cp.start()
             bk.append(cp)
             sent.append(cp)
 
-    lend(2)
-    lend(1)
-    send_back(2)
-    lend(3)
+    view_grad(0, 0)
+    view_grad(0, 1)
+    view_grad(1, 0)
+    for cp in load_w:
+        cp.wait()
+    for cp in lend_w:
+        cp.wait_recv()
+    send_back(0)
+    view_grad(1, 1)
     send_back(1)
-    lend(0)
-    send_back(3)
-    send_back(0)
+    for part in range(2):
+        keep[halves[part]] = back(part, 0)
+    load_p.wait()
     for cp in bk:
         cp.wait_recv()
     total = keep[...]
@@ -369,7 +383,7 @@
         total = total + bk_r[r].astype(F32)
     pg_out[...] = jnp.where(pab[...] > 0, total, 0.0).astype(BF16)
 
-    for cp in s1j + s1k[1:] + gj + gk[1:] + s2 + s3 + [share] + sent:
+    for cp in s1j + s1k[1:] + gj + gk[1:] + s2 + s3 + [share] + lend_w + sent:
         cp.wait_send()
 
     @pl.when(jnp.logical_not(diagonal))
@@ -378,7 +392,7 @@
         gk[0].wait_send()
 
 
-def on_device(first_view, second_view, weight, pre_act):
+def backward(first_view, second_view, weight, pre_act):
     dma = pltpu.SemaphoreType.DMA
     vmem = pltpu.VMEM
     return pl.pallas_call(
@@ -392,7 +406,7 @@
             vmem((4, ROWS, COLS), BF16),
             vmem((2, 4, ROWS, COLS), BF16),
             vmem((ROWS, COLS), BF16),
-            vmem((D, COLS), BF16),
+            vmem((4, 2, COLS, COLS), BF16),
             vmem((ROWS, COLS), BF16),
             vmem((1, COLS), F32),
             vmem((2, 4, 1, COLS), F32),
@@ -409,8 +423,7 @@
             vmem((2, 4, ROWS, COLS // 2), F32),
             vmem((2, 4, ROWS, COLS // 2), BF16),
             vmem((2, 4, ROWS, COLS // 2), BF16),
-            vmem((4, ROWS, COLS), BF16),
-            vmem((4, ROWS, COLS), BF16),
+            vmem((ROWS, COLS), BF16),
             vmem((4, ROWS, COLS), BF16),
             vmem((4, ROWS, COLS), BF16),
             vmem((ROWS, COLS), F32),
@@ -419,13 +432,38 @@
             dma((2, 4)), dma((2, 4)), dma((16,)), dma((16,)), dma((16,)), dma((16,)),
             dma, dma, dma((2, 2, 2, 4)), dma((2, 2, 2, 4)), dma((2, 2)), dma((2, 2)),
             dma((2, 2, 2, 4)), dma((2, 2, 2, 4)),
-            dma((2, 4)), dma((2, 4)), dma((4,)), dma((4,)), dma((4,)), dma((4,)),
+            dma((2, 4, 2)), dma((2, 4, 2)), dma((2, 2)), dma((2, 2)), dma((4, 2)), dma((4, 2)),
+            dma((4,)), dma((4,)), dma((4,)),
         ],
         compiler_params=pltpu.CompilerParams(
             collective_id=0, has_side_effects=True, vmem_limit_bytes=60 * 2**20),
         cost_estimate=pl.CostEstimate(flops=2700000000, bytes_accessed=5000000, transcendentals=0),
         name="vicreg_backward",
-    )(first_view, second_view, weight, pre_act)
+    )(first_view, second_view, weight.reshape(8, COLS, COLS), pre_act)
+
+
+def store_kernel(a, b, a_out, b_out, sems):
+    copies = []
+    for i in range(4):
+        rows = slice(i * 32, (i + 1) * 32)
+        copies.append(pltpu.make_async_copy(a.at[rows], a_out.at[rows], sems.at[0, i]))
+        copies.append(pltpu.make_async_copy(b.at[rows], b_out.at[rows], sems.at[1, i]))
+    for cp in copies:
+        cp.start()
+    for cp in copies:
+        cp.wait()
+
+
+def on_device(*args):
+    return pl.pallas_call(
+        store_kernel,
+        out_shape=[jax.ShapeDtypeStruct((ROWS, COLS), BF16)] * 2,
+        in_specs=[pl.BlockSpec(memory_space=pl.ANY)] * 2,
+        out_specs=[pl.BlockSpec(memory_space=pl.ANY)] * 2,
+        scratch_shapes=[pltpu.SemaphoreType.DMA((2, 4))],
+        compiler_params=pltpu.CompilerParams(vmem_limit_bytes=60 * 2**20),
+        name="store",
+    )(*backward(*args))
 
 
 def solution(mesh):

time: 92.8 us -> 98.2 us (1.058)
  the two profiles are of different devices: /device:TPU:17 before, /device:TPU:1 now
where the time goes in v3:
time: 98.2 us; the launch traced here: 96.7 us
  Pallas kernels  96 us (98%)
    pallas_call x1, Pallas kernels, backward(): pl.pallas_call(kernel, out_shape=[jax.ShapeDtypeStruct((ROWS, COLS), BF16...  86.9 us
    pallas_call x1, Pallas kernels, on_device(): pl.pallas_call(store_kernel, out_shape=[jax.ShapeDtypeStruct((ROWS, COLS)...  9.12 us

profile of v3, /device:TPU:1, one launch (start us, length us, event | category | flops | bytes accessed | tf_op | source)
XLA Modules:
  0.0 96.7 jit_solution(5885622067858937543)
XLA Ops:
  0.6 86.9 %vicreg_backward.1 = (bf16[128,512]{1,0:T(8,128)(2,1)}, bf16[128,512]{1,0:T(8,128)(2,1)}) custom-call(bf16[128,512]{1,0:T(8,128)(2,1)} %fv.1, bf16[128,512]{1,0:T(8,128)(2,1)} %sv.1, bf16[8,512,512]{2,1,0:T(8,128)(2,1)} %bitcast.1, bf16[128,512]{1,0:T(8,128)(2,1)} %pa.1), custom_call_target="tpu_custom_call" | custom-call | flops 2700000000 | bytes 5000000 | tf_op jit(solution)/shard_map/vicreg_backward/pallas_call | solution.py:398
  87.5 9.1 %store.1 = (bf16[128,512]{1,0:T(8,128)(2,1)}, bf16[128,512]{1,0:T(8,128)(2,1)}) custom-call(bf16[128,512]{1,0:T(8,128)(2,1)} %get-tuple-element.4.a, bf16[128,512]{1,0:T(8,128)(2,1)} %get-tuple-element.5.b), custom_call_target="tpu_custom_call" | custom-call | tf_op jit(solution)/shard_map/store/pallas_call | solution.py:458

commit v4 on v3

--- a/solution.py
+++ b/solution.py
@@ -8,7 +8,6 @@
 D = 4096
 N = 8192
 ROWS = 128
-HALF = 64
 COLS = 512
 UNIT = 32
 
@@ -223,24 +222,25 @@
         rs[q, h, way, k] = cp
         sent.append(cp)
 
+    def start_reduce(q, h):
+        for way in range(2):
+            reduce_step(q, h, way, 4)
+            reduce_step(q, h, way, 3)
+
     block(0)
-    for q in range(2):
-        for way in range(2):
-            reduce_step(q, 0, way, 4)
-            reduce_step(q, 0, way, 3)
+    start_reduce(0, 0)
     share.wait_recv()
     block(1)
-    for q in range(2):
-        for way in range(2):
-            reduce_step(q, 1, way, 4)
-            reduce_step(q, 1, way, 3)
-    for cp in s3:
-        cp.start()
+    start_reduce(0, 1)
+    start_reduce(1, 0)
+    start_reduce(1, 1)
     for k in (2, 1):
         for q in range(2):
             for h in range(2):
                 for way in range(2):
                     reduce_step(q, h, way, k)
+    for cp in s3:
+        cp.start()
 
     swap = {}
     for q in range(2):
@@ -277,14 +277,6 @@
             for way in range(2):
                 gather_step(q, h, way, 1)
 
-    for cp in s3:
-        cp.wait_recv()
-    variance = msq[...]
-    for r in range(1, 16):
-        variance = variance + st3[r]
-    variance = variance / (N - 1)
-    deviation = jnp.sqrt(variance + var_eps)
-    hinge = jnp.where(deviation < 1.0, 1.0, 0.0).astype(F32)
     for k in (2, 3):
         for q in range(2):
             for h in range(2):
@@ -293,8 +285,15 @@
                     if k == 3:
                         gather_step(q, h, way, 4)
 
+    for cp in s3:
+        cp.wait_recv()
+    variance = msq[...]
+    for r in range(1, 16):
+        variance = variance + st3[r]
+    variance = variance / (N - 1)
+    deviation = jnp.sqrt(variance + var_eps)
+    hinge = jnp.where(deviation < 1.0, 1.0, 0.0).astype(F32)
     cx = {}
-    halves = (slice(0, HALF), slice(HALF, ROWS))
 
     def product(q):
         for h in range(2):
@@ -309,72 +308,60 @@
             pk[1].reshape(4 * ROWS, COLS), call[1, q].reshape(COLS // 2, COLS), NT,
             preferred_element_type=F32)
         cov[q] = out.reshape(4, ROWS, COLS // 2)
-        for rows in ((slice(0, ROWS),) if q == 0 else halves):
-            part = rows.start // HALF
-            for r in (2, 1, 3):
-                cx_s[q, r, rows] = cov[q, (x + r) % 4, rows].astype(BF16)
-                cp = remote(cx_s.at[q, r, rows], cx_r.at[q, r, rows], cx_ss.at[q, r, part],
-                            cx_rs.at[q, r, part], to_x(r))
-                cp.start()
-                cx[q, r, part] = cp
-                sent.append(cp)
+        for r in (2, 1, 3):
+            cx_s[q, r] = cov[q, (x + r) % 4].astype(BF16)
+            cp = remote(cx_s.at[q, r], cx_r.at[q, r], cx_ss.at[q, r], cx_rs.at[q, r], to_x(r))
+            cp.start()
+            cx[q, r] = cp
+            sent.append(cp)
 
     product(0)
     product(1)
     load_s.wait()
     factor = N * D / loss_share
-    vgc = {}
-
-    def view_grad(q, part):
+    vgc = []
+
+    def view_grad(q):
         at = slice(q * COLS // 2, (q + 1) * COLS // 2)
-        rows = halves[part]
-        cov_prod = cov[q, x, rows]
+        cov_prod = cov[q, x]
         for r in range(1, 4):
-            if (q, r, part) in cx:
-                cx[q, r, part].wait_recv()
-            cov_prod = cov_prod + cx_r[q, r, rows].astype(F32)
-        values = xj[x, rows, at].astype(F32)
+            cx[q, r].wait_recv()
+            cov_prod = cov_prod + cx_r[q, r].astype(F32)
+        values = xj[x, :, at].astype(F32)
         centered = values - mean_j[:, at]
-        invariance = 2.0 * inv_weight / (N * D) * (values - svb[rows, at].astype(F32))
+        invariance = 2.0 * inv_weight / (N * D) * (values - svb[:, at].astype(F32))
         spread_term = -var_weight / D * hinge[:, at] * centered / ((N - 1) * deviation[:, at])
         cov_term = 4.0 * cov_weight / (D * (N - 1)) * (cov_prod / (N - 1) - centered * variance[:, at])
-        vg_out[rows, at] = (factor * (invariance + spread_term + cov_term)).astype(BF16)
-        cp = remote(vg_out.at[rows, at], vgp.at[rows, at], vg_ss.at[q, part], vg_rs.at[q, part], partner)
-        cp.start()
-        vgc[q, part] = cp
+        vg_out[:, at] = (factor * (invariance + spread_term + cov_term)).astype(BF16)
+        cp = remote(vg_out.at[:, at], vgp.at[:, at], vg_ss.at[q], vg_rs.at[q], partner)
+        cp.start()
+        vgc.append(cp)
         sent.append(cp)
 
+    view_grad(0)
+    view_grad(1)
+
     bk = []
 
-    def back(part, r):
-        rows = halves[part]
+    def back(r):
         at = (yl + r) % 4
-        out = lax.dot_general(vg_out[rows], wb[at, 0], NT, preferred_element_type=F32)
-        return out + lax.dot_general(vgp[rows], wb[at, 1], NT, preferred_element_type=F32)
-
-    def send_back(part):
-        rows = halves[part]
-        for q in range(2):
-            vgc[q, part].wait_recv()
-        for r in (2, 1, 3):
-            bk_s[r, rows] = back(part, r).astype(BF16)
-            cp = remote(bk_s.at[r, rows], bk_r.at[r, rows], bk_ss.at[r, part], bk_rs.at[r, part], to_yl(r))
-            cp.start()
-            bk.append(cp)
-            sent.append(cp)
-
-    view_grad(0, 0)
-    view_grad(0, 1)
-    view_grad(1, 0)
+        out = lax.dot_general(vg_out[...], wb[at, 0], NT, preferred_element_type=F32)
+        if r == 2:
+            for cp in vgc:
+                cp.wait_recv()
+        return out + lax.dot_general(vgp[...], wb[at, 1], NT, preferred_element_type=F32)
+
     for cp in load_w:
         cp.wait()
     for cp in lend_w:
         cp.wait_recv()
-    send_back(0)
-    view_grad(1, 1)
-    send_back(1)
-    for part in range(2):
-        keep[halves[part]] = back(part, 0)
+    for r in (2, 1, 3):
+        bk_s[r] = back(r).astype(BF16)
+        cp = remote(bk_s.at[r], bk_r.at[r], bk_ss.at[r], bk_rs.at[r], to_yl(r))
+        cp.start()
+        bk.append(cp)
+        sent.append(cp)
+    keep[...] = back(0)
     load_p.wait()
     for cp in bk:
         cp.wait_recv()
@@ -432,7 +419,7 @@
             dma((2, 4)), dma((2, 4)), dma((16,)), dma((16,)), dma((16,)), dma((16,)),
             dma, dma, dma((2, 2, 2, 4)), dma((2, 2, 2, 4)), dma((2, 2)), dma((2, 2)),
             dma((2, 2, 2, 4)), dma((2, 2, 2, 4)),
-            dma((2, 4, 2)), dma((2, 4, 2)), dma((2, 2)), dma((2, 2)), dma((4, 2)), dma((4, 2)),
+            dma((2, 4)), dma((2, 4)), dma((2,)), dma((2,)), dma((4,)), dma((4,)),
             dma((4,)), dma((4,)), dma((4,)),
         ],
         compiler_params=pltpu.CompilerParams(
@@ -442,25 +429,17 @@
     )(first_view, second_view, weight.reshape(8, COLS, COLS), pre_act)
 
 
-def store_kernel(a, b, a_out, b_out, sems):
-    copies = []
-    for i in range(4):
-        rows = slice(i * 32, (i + 1) * 32)
-        copies.append(pltpu.make_async_copy(a.at[rows], a_out.at[rows], sems.at[0, i]))
-        copies.append(pltpu.make_async_copy(b.at[rows], b_out.at[rows], sems.at[1, i]))
-    for cp in copies:
-        cp.start()
-    for cp in copies:
-        cp.wait()
+def store_kernel(a, b, a_out, b_out):
+    a_out[...] = a[...]
+    b_out[...] = b[...]
 
 
 def on_device(*args):
     return pl.pallas_call(
         store_kernel,
         out_shape=[jax.ShapeDtypeStruct((ROWS, COLS), BF16)] * 2,
-        in_specs=[pl.BlockSpec(memory_space=pl.ANY)] * 2,
-        out_specs=[pl.BlockSpec(memory_space=pl.ANY)] * 2,
-        scratch_shapes=[pltpu.SemaphoreType.DMA((2, 4))],
+        in_specs=[pl.BlockSpec(memory_space=pltpu.VMEM)] * 2,
+        out_specs=[pl.BlockSpec(memory_space=pltpu.VMEM)] * 2,
         compiler_params=pltpu.CompilerParams(vmem_limit_bytes=60 * 2**20),
         name="store",
     )(*backward(*args))

time: 98.2 us -> 91.9 us (0.936)
  Pallas kernels: 96 us -> 89.5 us
    pallas_call x1, Pallas kernels: 9.12 us -> 1.68 us  [on_device(): pl.pallas_call(store_kernel, out_shape=[jax.ShapeDtypeStruct((ROWS, COLS)...]
where the time goes in v4:
time: 91.9 us; the launch traced here: 90.1 us
  Pallas kernels  89.5 us (97%)
    pallas_call x1, Pallas kernels, backward(): pl.pallas_call(kernel, out_shape=[jax.ShapeDtypeStruct((ROWS, COLS), BF16...  87.8 us

profile of v4, /device:TPU:1, one launch (start us, length us, event | category | flops | bytes accessed | tf_op | source)
XLA Modules:
  0.0 90.1 jit_solution(11541299241829293660)
XLA Ops:
  0.6 87.8 %vicreg_backward.1 = (bf16[128,512]{1,0:T(8,128)(2,1)}, bf16[128,512]{1,0:T(8,128)(2,1)}) custom-call(bf16[128,512]{1,0:T(8,128)(2,1)} %fv.1, bf16[128,512]{1,0:T(8,128)(2,1)} %sv.1, bf16[8,512,512]{2,1,0:T(8,128)(2,1)} %bitcast.1, bf16[128,512]{1,0:T(8,128)(2,1)} %pa.1), custom_call_target="tpu_custom_call" | custom-call | flops 2700000000 | bytes 5000000 | tf_op jit(solution)/shard_map/vicreg_backward/pallas_call | solution.py:385
  88.5 1.7 %store.1 = (bf16[128,512]{1,0:T(8,128)(2,1)}, bf16[128,512]{1,0:T(8,128)(2,1)}) custom-call(bf16[128,512]{1,0:T(8,128)(2,1)} %get-tuple-element.4.a, bf16[128,512]{1,0:T(8,128)(2,1)} %get-tuple-element.5.b), custom_call_target="tpu_custom_call" | custom-call | tf_op jit(solution)/shard_map/store/pallas_call | solution.py:438

commit v5 on v4

v5 whole, which is shorter than its diff:
```python
import jax
import jax.numpy as jnp
from jax import lax
from jax.experimental import pallas as pl
from jax.experimental.pallas import tpu as pltpu
from jax.sharding import PartitionSpec as P

D = 4096
N = 8192
ROWS = 128
COLS = 512
UNIT = 64
HALF = 256
GROUP = 512

inv_weight = 25.0
var_weight = 25.0
cov_weight = 1.0
var_eps = 1e-05
loss_share = 32.0

F32 = jnp.float32
BF16 = jnp.bfloat16
NT = (((1,), (1,)), ((), ()))
TN = (((0,), (0,)), ((), ()))


def kernel(
    fv, sv, w, pa, vg_out, pg_out,
    xj, xk, pj, pk, svb, wb, pab,
    tot, st, dsj, dsk, dja, dkb, corr,
    cf, rs_s, rs_r, yh_s, yh_r, call,
    cov, cx_s, cx_r, vgp, bk_s, bk_r, keep,
    lsem,
    xj_ss, xj_rs, xk_ss, xk_rs, st_ss, st_rs, dk_ss, dk_rs,
    pk_ss, pk_rs, rsz_ss, rsz_rs, yh_ss, yh_rs, ag_ss, ag_rs,
    cx_ss, cx_rs, vg_ss, vg_rs, bk_ss, bk_rs, w_sem, w_ss, w_rs,
):
    p = lax.axis_index("pairs")
    d = lax.axis_index("dims")
    z, yh, x = p // 8, (p // 4) % 2, p % 4
    yl, c = d // 2, d % 2

    def dev(z_, yh_, x_, yl_, c_):
        return (z_ * 8 + yh_ * 4 + x_, yl_ * 2 + c_)

    def to_x(r):
        return dev(z, yh, (x + r) % 4, yl, c)

    def to_k(r):
        return dev(z, yh, yl, (x + r) % 4, c)

    def from_k(r):
        return dev(z, yh, (yl + 4 - r) % 4, x, c)

    def to_yl(r):
        return dev(z, yh, x, (yl + r) % 4, c)

    def to_zy(r):
        return dev((z + r % 8) % 8, (yh + r // 8) % 2, x, yl, c)

    partner = dev(z, yh, x, yl, 1 - c)
    diagonal = x == yl

    def remote(src, dst, ss, rs, to):
        return pltpu.make_async_remote_copy(
            src_ref=src, dst_ref=dst, send_sem=ss, recv_sem=rs,
            device_id=to, device_id_type=pl.DeviceIdType.MESH)

    cols = (slice(0, HALF), slice(HALF, COLS))

    load_x = pltpu.make_async_copy(fv, xj.at[x], lsem.at[0])
    load_x.start()
    load_w = [
        pltpu.make_async_copy(w.at[i * 2 + c], wb.at[i, 0], w_sem.at[i]) for i in range(4)]
    load_s = pltpu.make_async_copy(sv, svb, lsem.at[2])
    load_p = pltpu.make_async_copy(pa, pab, lsem.at[3])
    load_k = [
        pltpu.make_async_copy(fv.at[:, cols[i]], xk.at[i, x], lsem.at[4 + i]) for i in range(2)]

    barrier = pltpu.get_barrier_semaphore()

    def greet(to):
        pl.semaphore_signal(barrier, inc=1, device_id=to, device_id_type=pl.DeviceIdType.MESH)

    count = 0
    for r in range(1, 16):
        greet(to_zy(r))
        count += 1
    for r in range(1, 4):
        greet(to_x(r))
        greet(to_k(r))
        greet(from_k(r))
        greet(to_yl(r))
        count += 4
    greet(partner)
    count += 1

    @pl.when(jnp.logical_not(diagonal))
    def _():
        greet(to_k(0))
        greet(from_k(0))

    @pl.when(diagonal)
    def _():
        for cp in load_k:
            cp.start()

    for cp in load_w:
        cp.start()
    load_s.start()
    load_p.start()
    load_x.wait()

    @pl.when(jnp.logical_not(diagonal))
    def _():
        pl.semaphore_wait(barrier, count + 2)

    @pl.when(diagonal)
    def _():
        pl.semaphore_wait(barrier, count)

    gj = [remote(xj.at[x], xj.at[x], xj_ss.at[r], xj_rs.at[r], to_x(r)) for r in range(1, 4)]
    gk = [[remote(xj.at[x, :, cols[i]], xk.at[i, x], xk_ss.at[i, r], xk_rs.at[i, r], to_k(r))
           for r in range(4)] for i in range(2)]

    def send_k(i):
        for cp in gk[i][1:]:
            cp.start()

        @pl.when(jnp.logical_not(diagonal))
        def _():
            gk[i][0].start()

    send_k(0)
    for cp in gj:
        cp.start()
    send_k(1)

    lend_w = [
        remote(w.at[i * 2 + 1 - c], wb.at[i, 1], w_ss.at[i], w_rs.at[i], partner) for i in range(4)]
    for cp in lend_w:
        cp.start()

    share = []

    def centre_k(i):
        for cp in gk[i][1:]:
            cp.wait_recv()

        @pl.when(jnp.logical_not(diagonal))
        def _():
            gk[i][0].wait_recv()

        @pl.when(diagonal)
        def _():
            load_k[i].wait()

        total = jnp.zeros((1, HALF), F32)
        for b in range(4):
            total = total + jnp.sum(xk[i, b].astype(F32), axis=0, keepdims=True)
        tot[2, :, cols[i]] = total
        for b in range(4):
            pk[0, i, b] = (xk[i, b].astype(F32) - total / GROUP).astype(BF16)
        cp = remote(pk.at[0, i], pk.at[1, i], pk_ss.at[i], pk_rs.at[i], partner)
        cp.start()
        share.append(cp)

    def centre_j():
        for cp in gj:
            cp.wait_recv()
        total = jnp.zeros((1, COLS), F32)
        for b in range(4):
            total = total + jnp.sum(xj[b].astype(F32), axis=0, keepdims=True)
        squares = jnp.zeros((1, COLS), F32)
        for b in range(4):
            centered = xj[b].astype(F32) - total / GROUP
            pj[b] = centered.astype(BF16)
            squares = squares + jnp.sum(centered * centered, axis=0, keepdims=True)
        tot[0] = total
        tot[1] = squares

    def block(i, h):
        prod = lax.dot_general(
            pj[...].reshape(GROUP, COLS), pk[h, i].reshape(GROUP, HALF), TN,
            preferred_element_type=F32)
        cf[i, h] = prod.reshape(8, UNIT, HALF)

    def along(way, hops):
        return dev((z + (hops if way == 0 else 8 - hops)) % 8, yh, x, yl, c)

    def unit(way, hops):
        return (z + (hops if way == 0 else 8 - hops)) % 8

    sent = []
    rs = {}

    def reduce_step(i, h, way, k):
        if k == 4 and h != way:
            return
        val = cf[i, h, unit(way, k)]
        for m in {2: (4, 3), 1: (2,)}.get(k, ()):
            if (i, h, way, m) in rs:
                rs[i, h, way, m].wait_recv()
                val = val + rs_r[i, h, way, m - 1].astype(F32)
        at = (i, h, way, k - 1)
        rs_s[at] = val.astype(BF16)
        cp = remote(rs_s.at[at], rs_r.at[at], rsz_ss.at[at], rsz_rs.at[at],
                    along(way, 2 if k == 4 else 1))
        cp.start()
        rs[i, h, way, k] = cp
        sent.append(cp)

    def start_reduce(i, h):
        for way in range(2):
            reduce_step(i, h, way, 4)
            reduce_step(i, h, way, 3)

    def reduce_all(i, k):
        for h in range(2):
            for way in range(2):
                reduce_step(i, h, way, k)

    swap = {}

    def swap_out(i):
        for h in range(2):
            mine = cf[i, h, z]
            for way in range(2):
                rs[i, h, way, 1].wait_recv()
                mine = mine + rs_r[i, h, way, 0].astype(F32)
            cf[i, h, z] = mine
            yh_s[i, h] = mine.astype(BF16)
            cp = remote(yh_s.at[i, h], yh_r.at[i, h], yh_ss.at[i, h], yh_rs.at[i, h], to_zy(8))
            cp.start()
            swap[i, h] = cp
            sent.append(cp)

    ag = {}

    def gather_step(i, h, way, k):
        if k == 4 and h != way:
            return
        if k > 1 and k != 4:
            ag[i, h, way, k - 1].wait_recv()
        at = (i, h, way, k - 1)
        held = call.at[i, h, unit(1 - way, min(k, 3) - 1)]
        cp = remote(held, held, ag_ss.at[at], ag_rs.at[at], along(way, 2 if k == 4 else 1))
        cp.start()
        ag[i, h, way, k] = cp
        sent.append(cp)

    def gather_first(i):
        for h in range(2):
            swap[i, h].wait_recv()
            full = cf[i, h, z] + yh_r[i, h].astype(F32) + corr[h, z, :, cols[i]]
            call[i, h, z] = full.astype(BF16)
            for way in range(2):
                gather_step(i, h, way, 1)

    def gather_all(i, k):
        for h in range(2):
            for way in range(2):
                gather_step(i, h, way, k)
                if k == 3:
                    gather_step(i, h, way, 4)

    def gather_wait(i):
        for h in range(2):
            for way in range(2):
                ag[i, h, way, 3].wait_recv()
            ag[i, h, h, 4].wait_recv()

    centre_k(0)
    centre_j()
    block(0, 0)
    start_reduce(0, 0)
    share[0].wait_recv()
    block(0, 1)
    start_reduce(0, 1)
    centre_k(1)
    block(1, 0)
    start_reduce(1, 0)
    share[1].wait_recv()
    block(1, 1)
    start_reduce(1, 1)

    s2 = [remote(tot, st.at[r], st_ss.at[r], st_rs.at[r], to_zy(r)) for r in range(1, 16)]
    for cp in s2:
        cp.start()
    reduce_all(0, 2)
    reduce_all(0, 1)
    reduce_all(1, 2)
    swap_out(0)
    reduce_all(1, 1)

    for cp in s2:
        cp.wait_recv()
    sums = tot[...]
    for r in range(1, 16):
        sums = sums + st[r]
    mean_j, mean_k = sums[0] / N, sums[2] / N
    for r in range(16):
        own = tot[...] if r == 0 else st[r]
        dsj[r:r + 1, :] = own[0] / GROUP - mean_j
        dsk[r:r + 1, :] = own[2] / GROUP - mean_k
    gap_j, gap_k = dsj[...], dsk[...]
    variance = (sums[1] + GROUP * jnp.sum(gap_j * gap_j, axis=0, keepdims=True)) / (N - 1)
    deviation = jnp.sqrt(variance + var_eps)
    hinge = jnp.where(deviation < 1.0, 1.0, 0.0).astype(F32)

    def split(value):
        high = value.astype(BF16)
        return high, (value - high.astype(F32)).astype(BF16)

    high, low = split(GROUP * gap_j)
    dja[0:16], dja[16:32], dja[32:48] = high, high, low
    high, low = split(gap_k)
    dkb[0, 0:16], dkb[0, 16:32], dkb[0, 32:48] = high, low, high
    share_d = remote(dkb.at[0], dkb.at[1], dk_ss, dk_rs, partner)
    share_d.start()

    def correction(h):
        corr[h] = lax.dot_general(
            dja[...], dkb[h], TN, preferred_element_type=F32).reshape(8, UNIT, COLS)

    correction(0)
    swap_out(1)
    share_d.wait_recv()
    correction(1)
    gather_first(0)

    for i in range(2):
        share[i].wait_send()
        for h in range(2):
            shift = dkb[h, 0:16].astype(F32)[0:1] + dkb[h, 16:32].astype(F32)[0:1]
            for b in range(4):
                pk[h, i, b] = (pk[h, i, b].astype(F32) + shift[:, cols[i]]).astype(BF16)
    gather_all(0, 2)
    gather_first(1)
    gather_all(0, 3)
    gather_all(1, 2)
    gather_all(1, 3)

    cx = {}

    def product(i, q):
        out = None
        for h in range(2):
            part = lax.dot_general(
                pk[h, i].reshape(GROUP, HALF), call[i, h, 4 * q:4 * q + 4].reshape(HALF, HALF), NT,
                preferred_element_type=F32)
            out = part if out is None else out + part
        return out.reshape(4, ROWS, HALF)

    gather_wait(0)
    for q in range(2):
        cov[q] = product(0, q)
    gather_wait(1)
    for q in range(2):
        cov[q] += product(1, q)
        for r in (2, 1, 3):
            cx_s[q, r] = cov[q, (x + r) % 4].astype(BF16)
            cp = remote(cx_s.at[q, r], cx_r.at[q, r], cx_ss.at[q, r], cx_rs.at[q, r], to_x(r))
            cp.start()
            cx[q, r] = cp
            sent.append(cp)

    load_s.wait()
    factor = N * D / loss_share
    vgc = []

    def view_grad(q):
        at = slice(q * HALF, (q + 1) * HALF)
        cov_prod = cov[q, x]
        for r in range(1, 4):
            cx[q, r].wait_recv()
            cov_prod = cov_prod + cx_r[q, r].astype(F32)
        values = xj[x, :, at].astype(F32)
        centered = values - mean_j[:, at]
        invariance = 2.0 * inv_weight / (N * D) * (values - svb[:, at].astype(F32))
        spread_term = -var_weight / D * hinge[:, at] * centered / ((N - 1) * deviation[:, at])
        cov_term = 4.0 * cov_weight / (D * (N - 1)) * (cov_prod / (N - 1) - centered * variance[:, at])
        vg_out[:, at] = (factor * (invariance + spread_term + cov_term)).astype(BF16)
        cp = remote(vg_out.at[:, at], vgp.at[:, at], vg_ss.at[q], vg_rs.at[q], partner)
        cp.start()
        vgc.append(cp)
        sent.append(cp)

    view_grad(0)
    view_grad(1)

    bk = []

    def back(r):
        at = (yl + r) % 4
        out = lax.dot_general(vg_out[...], wb[at, 0], NT, preferred_element_type=F32)
        if r == 2:
            for cp in vgc:
                cp.wait_recv()
        return out + lax.dot_general(vgp[...], wb[at, 1], NT, preferred_element_type=F32)

    for cp in load_w:
        cp.wait()
    for cp in lend_w:
        cp.wait_recv()
    for r in (2, 1, 3):
        bk_s[r] = back(r).astype(BF16)
        cp = remote(bk_s.at[r], bk_r.at[r], bk_ss.at[r], bk_rs.at[r], to_yl(r))
        cp.start()
        bk.append(cp)
        sent.append(cp)
    keep[...] = back(0)
    load_p.wait()
    for cp in bk:
        cp.wait_recv()
    total = keep[...]
    for r in range(1, 4):
        total = total + bk_r[r].astype(F32)
    pg_out[...] = jnp.where(pab[...] > 0, total, 0.0).astype(BF16)

    for cp in gj + gk[0][1:] + gk[1][1:] + s2 + [share_d] + lend_w + sent:
        cp.wait_send()

    @pl.when(jnp.logical_not(diagonal))
    def _():
        gk[0][0].wait_send()
        gk[1][0].wait_send()


def backward(first_view, second_view, weight, pre_act):
    dma = pltpu.SemaphoreType.DMA
    vmem = pltpu.VMEM
    return pl.pallas_call(
        kernel,
        out_shape=[jax.ShapeDtypeStruct((ROWS, COLS), BF16)] * 2,
        in_specs=[pl.BlockSpec(memory_space=pltpu.HBM)] * 4,
        out_specs=[pl.BlockSpec(memory_space=pltpu.VMEM)] * 2,
        scratch_shapes=[
            vmem((4, ROWS, COLS), BF16),
            vmem((2, 4, ROWS, HALF), BF16),
            vmem((4, ROWS, COLS), BF16),
            vmem((2, 2, 4, ROWS, HALF), BF16),
            vmem((ROWS, COLS), BF16),
            vmem((4, 2, COLS, COLS), BF16),
            vmem((ROWS, COLS), BF16),
            vmem((3, 1, COLS), F32),
            vmem((16, 3, 1, COLS), F32),
            vmem((16, COLS), F32),
            vmem((16, COLS), F32),
            vmem((48, COLS), BF16),
            vmem((2, 48, COLS), BF16),
            vmem((2, 8, UNIT, COLS), F32),
            vmem((2, 2, 8, UNIT, HALF), F32),
            vmem((2, 2, 2, 4, UNIT, HALF), BF16),
            vmem((2, 2, 2, 4, UNIT, HALF), BF16),
            vmem((2, 2, UNIT, HALF), BF16),
            vmem((2, 2, UNIT, HALF), BF16),
            vmem((2, 2, 8, UNIT, HALF), BF16),
            vmem((2, 4, ROWS, HALF), F32),
            vmem((2, 4, ROWS, HALF), BF16),
            vmem((2, 4, ROWS, HALF), BF16),
            vmem((ROWS, COLS), BF16),
            vmem((4, ROWS, COLS), BF16),
            vmem((4, ROWS, COLS), BF16),
            vmem((ROWS, COLS), F32),
            dma((6,)),
            dma((4,)), dma((4,)), dma((2, 4)), dma((2, 4)), dma((16,)), dma((16,)), dma, dma,
            dma((2,)), dma((2,)), dma((2, 2, 2, 4)), dma((2, 2, 2, 4)), dma((2, 2)), dma((2, 2)),
            dma((2, 2, 2, 4)), dma((2, 2, 2, 4)),
            dma((2, 4)), dma((2, 4)), dma((2,)), dma((2,)), dma((4,)), dma((4,)),
            dma((4,)), dma((4,)), dma((4,)),
        ],
        compiler_params=pltpu.CompilerParams(
            collective_id=0, has_side_effects=True, vmem_limit_bytes=60 * 2**20),
        cost_estimate=pl.CostEstimate(flops=2700000000, bytes_accessed=5000000, transcendentals=0),
        name="vicreg_backward",
    )(first_view, second_view, weight.reshape(8, COLS, COLS), pre_act)


def store_kernel(a, b, a_out, b_out):
    a_out[...] = a[...]
    b_out[...] = b[...]


def on_device(*args):
    return pl.pallas_call(
        store_kernel,
        out_shape=[jax.ShapeDtypeStruct((ROWS, COLS), BF16)] * 2,
        in_specs=[pl.BlockSpec(memory_space=pltpu.VMEM)] * 2,
        out_specs=[pl.BlockSpec(memory_space=pltpu.VMEM)] * 2,
        compiler_params=pltpu.CompilerParams(vmem_limit_bytes=60 * 2**20),
        name="store",
    )(*backward(*args))


def solution(mesh):
    return jax.shard_map(
        on_device,
        mesh=mesh,
        in_specs=(P("pairs", "dims"), P("pairs", "dims"), P(None, "dims"), P("pairs", "dims")),
        out_specs=(P("pairs", "dims"), P("pairs", "dims")),
        check_vma=False,
    )
```

time: 91.9 us -> 92.3 us (level)
  no operation moved by 1% of the time
where the time goes in v5:
time: 92.3 us; the launch traced here: 90.6 us
  Pallas kernels  90 us (98%)
    pallas_call x1, Pallas kernels, backward(): pl.pallas_call(kernel, out_shape=[jax.ShapeDtypeStruct((ROWS, COLS), BF16...  88.3 us

profile of v5, /device:TPU:1, one launch (start us, length us, event | category | flops | bytes accessed | tf_op | source)
XLA Modules:
  0.0 90.6 jit_solution(15540573977102918292)
XLA Ops:
  0.6 88.3 %vicreg_backward.1 = (bf16[128,512]{1,0:T(8,128)(2,1)}, bf16[128,512]{1,0:T(8,128)(2,1)}) custom-call(bf16[128,512]{1,0:T(8,128)(2,1)} %fv.1, bf16[128,512]{1,0:T(8,128)(2,1)} %sv.1, bf16[8,512,512]{2,1,0:T(8,128)(2,1)} %bitcast.1, bf16[128,512]{1,0:T(8,128)(2,1)} %pa.1), custom_call_target="tpu_custom_call" | custom-call | flops 2700000000 | bytes 5000000 | tf_op jit(solution)/shard_map/vicreg_backward/pallas_call | solution.py:434
  88.9 1.7 %store.1 = (bf16[128,512]{1,0:T(8,128)(2,1)}, bf16[128,512]{1,0:T(8,128)(2,1)}) custom-call(bf16[128,512]{1,0:T(8,128)(2,1)} %get-tuple-element.4.a, bf16[128,512]{1,0:T(8,128)(2,1)} %get-tuple-element.5.b), custom_call_target="tpu_custom_call" | custom-call | tf_op jit(solution)/shard_map/store/pallas_call | solution.py:487

commit v6 on v5

--- a/solution.py
+++ b/solution.py
@@ -184,7 +184,7 @@
         prod = lax.dot_general(
             pj[...].reshape(GROUP, COLS), pk[h, i].reshape(GROUP, HALF), TN,
             preferred_element_type=F32)
-        cf[i, h] = prod.reshape(8, UNIT, HALF)
+        cf[i, :, h] = prod.reshape(8, UNIT, HALF)
 
     def along(way, hops):
         return dev((z + (hops if way == 0 else 8 - hops)) % 8, yh, x, yl, c)
@@ -195,100 +195,96 @@
     sent = []
     rs = {}
 
-    def reduce_step(i, h, way, k):
-        if k == 4 and h != way:
-            return
-        val = cf[i, h, unit(way, k)]
-        for m in {2: (4, 3), 1: (2,)}.get(k, ()):
-            if (i, h, way, m) in rs:
-                rs[i, h, way, m].wait_recv()
-                val = val + rs_r[i, h, way, m - 1].astype(F32)
-        at = (i, h, way, k - 1)
-        rs_s[at] = val.astype(BF16)
-        cp = remote(rs_s.at[at], rs_r.at[at], rsz_ss.at[at], rsz_rs.at[at],
+    def reduce_step(i, way, k):
+        at = unit(way, k)
+        if k == 4:
+            held, land = rs_s.at[i, way, 3, way], rs_r.at[i, way, 3, way]
+            rs_s[i, way, 3, way] = cf[i, at, way].astype(BF16)
+        else:
+            held, land = rs_s.at[i, way, k - 1], rs_r.at[i, way, k - 1]
+            if k == 2:
+                rs[i, way, 4].wait_recv()
+            if k < 3:
+                rs[i, way, k + 1].wait_recv()
+            for h in range(2):
+                val = cf[i, at, h]
+                if k == 2 and h == way:
+                    val = val + rs_r[i, way, 3, h].astype(F32)
+                if k < 3:
+                    val = val + rs_r[i, way, k, h].astype(F32)
+                rs_s[i, way, k - 1, h] = val.astype(BF16)
+        cp = remote(held, land, rsz_ss.at[i, way, k - 1], rsz_rs.at[i, way, k - 1],
                     along(way, 2 if k == 4 else 1))
         cp.start()
-        rs[i, h, way, k] = cp
+        rs[i, way, k] = cp
         sent.append(cp)
 
-    def start_reduce(i, h):
+    def reduce_all(i, *steps):
+        for k in steps:
+            for way in range(2):
+                reduce_step(i, way, k)
+
+    swap = {}
+
+    def swap_out(i):
         for way in range(2):
-            reduce_step(i, h, way, 4)
-            reduce_step(i, h, way, 3)
-
-    def reduce_all(i, k):
+            rs[i, way, 1].wait_recv()
         for h in range(2):
+            mine = cf[i, z, h] + rs_r[i, 0, 0, h].astype(F32) + rs_r[i, 1, 0, h].astype(F32)
+            cf[i, z, h] = mine
+            yh_s[i, h] = mine.astype(BF16)
+        cp = remote(yh_s.at[i], yh_r.at[i], yh_ss.at[i], yh_rs.at[i], to_zy(8))
+        cp.start()
+        swap[i] = cp
+        sent.append(cp)
+
+    ag = {}
+
+    def gather_step(i, way, k):
+        if k in (2, 4):
+            ag[i, way, k // 2].wait_recv()
+        held = call.at[i, unit(1 - way, min(k, 3) - 1)]
+        if k == 4:
+            held = call.at[i, unit(1 - way, 2), way]
+        cp = remote(held, held, ag_ss.at[i, way, k - 1], ag_rs.at[i, way, k - 1],
+                    along(way, 2 if k == 4 else 1))
+        cp.start()
+        ag[i, way, k] = cp
+        sent.append(cp)
+
+    def gather_first(i):
+        swap[i].wait_recv()
+        for h in range(2):
+            full = cf[i, z, h] + yh_r[i, h].astype(F32) + corr[h, z, :, cols[i]]
+            call[i, z, h] = full.astype(BF16)
+        gather_all(i, 1)
+
+    def gather_all(i, *steps):
+        for k in steps:
             for way in range(2):
-                reduce_step(i, h, way, k)
-
-    swap = {}
-
-    def swap_out(i):
-        for h in range(2):
-            mine = cf[i, h, z]
-            for way in range(2):
-                rs[i, h, way, 1].wait_recv()
-                mine = mine + rs_r[i, h, way, 0].astype(F32)
-            cf[i, h, z] = mine
-            yh_s[i, h] = mine.astype(BF16)
-            cp = remote(yh_s.at[i, h], yh_r.at[i, h], yh_ss.at[i, h], yh_rs.at[i, h], to_zy(8))
-            cp.start()
-            swap[i, h] = cp
-            sent.append(cp)
-
-    ag = {}
-
-    def gather_step(i, h, way, k):
-        if k == 4 and h != way:
-            return
-        if k > 1 and k != 4:
-            ag[i, h, way, k - 1].wait_recv()
-        at = (i, h, way, k - 1)
-        held = call.at[i, h, unit(1 - way, min(k, 3) - 1)]
-        cp = remote(held, held, ag_ss.at[at], ag_rs.at[at], along(way, 2 if k == 4 else 1))
-        cp.start()
-        ag[i, h, way, k] = cp
-        sent.append(cp)
-
-    def gather_first(i):
-        for h in range(2):
-            swap[i, h].wait_recv()
-            full = cf[i, h, z] + yh_r[i, h].astype(F32) + corr[h, z, :, cols[i]]
-            call[i, h, z] = full.astype(BF16)
-            for way in range(2):
-                gather_step(i, h, way, 1)
-
-    def gather_all(i, k):
-        for h in range(2):
-            for way in range(2):
-                gather_step(i, h, way, k)
-                if k == 3:
-                    gather_step(i, h, way, 4)
+                gather_step(i, way, k)
 
     def gather_wait(i):
-        for h in range(2):
-            for way in range(2):
-                ag[i, h, way, 3].wait_recv()
-            ag[i, h, h, 4].wait_recv()
+        for way in range(2):
+            ag[i, way, 3].wait_recv()
+            ag[i, way, 4].wait_recv()
 
     centre_k(0)
     centre_j()
     block(0, 0)
-    start_reduce(0, 0)
     share[0].wait_recv()
     block(0, 1)
-    start_reduce(0, 1)
+    reduce_all(0, 4, 3)
     centre_k(1)
     block(1, 0)
-    start_reduce(1, 0)
     share[1].wait_recv()
     block(1, 1)
-    start_reduce(1, 1)
+    reduce_all(1, 4, 3)
+    reduce_all(0, 2)
 
     s2 = [remote(tot, st.at[r], st_ss.at[r], st_rs.at[r], to_zy(r)) for r in range(1, 16)]
     for cp in s2:
         cp.start()
-    reduce_all(0, 2)
     reduce_all(0, 1)
     reduce_all(1, 2)
     swap_out(0)
@@ -338,9 +334,9 @@
                 pk[h, i, b] = (pk[h, i, b].astype(F32) + shift[:, cols[i]]).astype(BF16)
     gather_all(0, 2)
     gather_first(1)
-    gather_all(0, 3)
+    gather_all(0, 4, 3)
     gather_all(1, 2)
-    gather_all(1, 3)
+    gather_all(1, 4, 3)
 
     cx = {}
 
@@ -348,7 +344,7 @@
         out = None
         for h in range(2):
             part = lax.dot_general(
-                pk[h, i].reshape(GROUP, HALF), call[i, h, 4 * q:4 * q + 4].reshape(HALF, HALF), NT,
+                pk[h, i].reshape(GROUP, HALF), call[i, 4 * q:4 * q + 4, h].reshape(HALF, HALF), NT,
                 preferred_element_type=F32)
             out = part if out is None else out + part
         return out.reshape(4, ROWS, HALF)
@@ -451,12 +447,12 @@
             vmem((48, COLS), BF16),
             vmem((2, 48, COLS), BF16),
             vmem((2, 8, UNIT, COLS), F32),
-            vmem((2, 2, 8, UNIT, HALF), F32),
-            vmem((2, 2, 2, 4, UNIT, HALF), BF16),
-            vmem((2, 2, 2, 4, UNIT, HALF), BF16),
+            vmem((2, 8, 2, UNIT, HALF), F32),
+            vmem((2, 2, 4, 2, UNIT, HALF), BF16),
+            vmem((2, 2, 4, 2, UNIT, HALF), BF16),
             vmem((2, 2, UNIT, HALF), BF16),
             vmem((2, 2, UNIT, HALF), BF16),
-            vmem((2, 2, 8, UNIT, HALF), BF16),
+            vmem((2, 8, 2, UNIT, HALF), BF16),
             vmem((2, 4, ROWS, HALF), F32),
             vmem((2, 4, ROWS, HALF), BF16),
             vmem((2, 4, ROWS, HALF), BF16),
@@ -466,8 +462,8 @@
             vmem((ROWS, COLS), F32),
             dma((6,)),
             dma((4,)), dma((4,)), dma((2, 4)), dma((2, 4)), dma((16,)), dma((16,)), dma, dma,
-            dma((2,)), dma((2,)), dma((2, 2, 2, 4)), dma((2, 2, 2, 4)), dma((2, 2)), dma((2, 2)),
-            dma((2, 2, 2, 4)), dma((2, 2, 2, 4)),
+            dma((2,)), dma((2,)), dma((2, 2, 4)), dma((2, 2, 4)), dma((2,)), dma((2,)),
+            dma((2, 2, 4)), dma((2, 2, 4)),
             dma((2, 4)), dma((2, 4)), dma((2,)), dma((2,)), dma((4,)), dma((4,)),
             dma((4,)), dma((4,)), dma((4,)),
         ],

time: 92.3 us -> 93 us (level)
  no operation moved by 1% of the time
where the time goes in v6:
time: 93 us; the launch traced here: 91.2 us
  Pallas kernels  90.6 us (97%)
    pallas_call x1, Pallas kernels, backward(): pl.pallas_call(kernel, out_shape=[jax.ShapeDtypeStruct((ROWS, COLS), BF16...  88.9 us

profile of v6, /device:TPU:1, one launch (start us, length us, event | category | flops | bytes accessed | tf_op | source)
XLA Modules:
  0.0 91.2 jit_solution(12906264636001407284)
XLA Ops:
  0.6 88.9 %vicreg_backward.1 = (bf16[128,512]{1,0:T(8,128)(2,1)}, bf16[128,512]{1,0:T(8,128)(2,1)}) custom-call(bf16[128,512]{1,0:T(8,128)(2,1)} %fv.1, bf16[128,512]{1,0:T(8,128)(2,1)} %sv.1, bf16[8,512,512]{2,1,0:T(8,128)(2,1)} %bitcast.1, bf16[128,512]{1,0:T(8,128)(2,1)} %pa.1), custom_call_target="tpu_custom_call" | custom-call | flops 2700000000 | bytes 5000000 | tf_op jit(solution)/shard_map/vicreg_backward/pallas_call | solution.py:430
  89.5 1.7 %store.1 = (bf16[128,512]{1,0:T(8,128)(2,1)}, bf16[128,512]{1,0:T(8,128)(2,1)}) custom-call(bf16[128,512]{1,0:T(8,128)(2,1)} %get-tuple-element.4.a, bf16[128,512]{1,0:T(8,128)(2,1)} %get-tuple-element.5.b), custom_call_target="tpu_custom_call" | custom-call | tf_op jit(solution)/shard_map/store/pallas_call | solution.py:483

commit v7 on v6

--- a/solution.py
+++ b/solution.py
@@ -30,7 +30,7 @@
     xj, xk, pj, pk, svb, wb, pab,
     tot, st, dsj, dsk, dja, dkb, corr,
     cf, rs_s, rs_r, yh_s, yh_r, call,
-    cov, cx_s, cx_r, vgp, bk_s, bk_r, keep,
+    cov, cx_s, cx_r, vgs, vgp, bk_s, bk_r, keep,
     lsem,
     xj_ss, xj_rs, xk_ss, xk_rs, st_ss, st_rs, dk_ss, dk_rs,
     pk_ss, pk_rs, rsz_ss, rsz_rs, yh_ss, yh_rs, ag_ss, ag_rs,
@@ -276,15 +276,15 @@
     block(0, 1)
     reduce_all(0, 4, 3)
     centre_k(1)
+
+    s2 = [remote(tot, st.at[r], st_ss.at[r], st_rs.at[r], to_zy(r)) for r in range(1, 16)]
+    for cp in s2:
+        cp.start()
     block(1, 0)
     share[1].wait_recv()
     block(1, 1)
     reduce_all(1, 4, 3)
     reduce_all(0, 2)
-
-    s2 = [remote(tot, st.at[r], st_ss.at[r], st_rs.at[r], to_zy(r)) for r in range(1, 16)]
-    for cp in s2:
-        cp.start()
     reduce_all(0, 1)
     reduce_all(1, 2)
     swap_out(0)
@@ -320,11 +320,10 @@
         corr[h] = lax.dot_general(
             dja[...], dkb[h], TN, preferred_element_type=F32).reshape(8, UNIT, COLS)
 
+    swap_out(1)
     correction(0)
-    swap_out(1)
     share_d.wait_recv()
     correction(1)
-    gather_first(0)
 
     for i in range(2):
         share[i].wait_send()
@@ -332,6 +331,7 @@
             shift = dkb[h, 0:16].astype(F32)[0:1] + dkb[h, 16:32].astype(F32)[0:1]
             for b in range(4):
                 pk[h, i, b] = (pk[h, i, b].astype(F32) + shift[:, cols[i]]).astype(BF16)
+    gather_first(0)
     gather_all(0, 2)
     gather_first(1)
     gather_all(0, 4, 3)
@@ -377,8 +377,8 @@
         invariance = 2.0 * inv_weight / (N * D) * (values - svb[:, at].astype(F32))
         spread_term = -var_weight / D * hinge[:, at] * centered / ((N - 1) * deviation[:, at])
         cov_term = 4.0 * cov_weight / (D * (N - 1)) * (cov_prod / (N - 1) - centered * variance[:, at])
-        vg_out[:, at] = (factor * (invariance + spread_term + cov_term)).astype(BF16)
-        cp = remote(vg_out.at[:, at], vgp.at[:, at], vg_ss.at[q], vg_rs.at[q], partner)
+        vgs[q] = (factor * (invariance + spread_term + cov_term)).astype(BF16)
+        cp = remote(vgs.at[q], vgp.at[q], vg_ss.at[q], vg_rs.at[q], partner)
         cp.start()
         vgc.append(cp)
         sent.append(cp)
@@ -390,11 +390,14 @@
 
     def back(r):
         at = (yl + r) % 4
-        out = lax.dot_general(vg_out[...], wb[at, 0], NT, preferred_element_type=F32)
-        if r == 2:
-            for cp in vgc:
-                cp.wait_recv()
-        return out + lax.dot_general(vgp[...], wb[at, 1], NT, preferred_element_type=F32)
+        out = None
+        for core, held in enumerate((vgs, vgp)):
+            for q in range(2):
+                if core == 1 and r == 2:
+                    vgc[q].wait_recv()
+                part = lax.dot_general(held[q], wb[at, core, :, cols[q]], NT, preferred_element_type=F32)
+                out = part if out is None else out + part
+        return out
 
     for cp in load_w:
         cp.wait()
@@ -407,6 +410,8 @@
         bk.append(cp)
         sent.append(cp)
     keep[...] = back(0)
+    for q in range(2):
+        vg_out[:, cols[q]] = vgs[q]
     load_p.wait()
     for cp in bk:
         cp.wait_recv()
@@ -456,7 +461,8 @@
             vmem((2, 4, ROWS, HALF), F32),
             vmem((2, 4, ROWS, HALF), BF16),
             vmem((2, 4, ROWS, HALF), BF16),
-            vmem((ROWS, COLS), BF16),
+            vmem((2, ROWS, HALF), BF16),
+            vmem((2, ROWS, HALF), BF16),
             vmem((4, ROWS, COLS), BF16),
             vmem((4, ROWS, COLS), BF16),
             vmem((ROWS, COLS), F32),

time: 93 us -> 93.8 us (level); the launches traced: 91.2 us -> 93.4 us
  Pallas kernels: 90.6 us -> 92.7 us
    pallas_call x1, Pallas kernels: 88.9 us -> 91.1 us  [backward(): pl.pallas_call(kernel, out_shape=[jax.ShapeDtypeStruct((ROWS, COLS), BF16...]
where the time goes in v7:
time: 93.8 us; the launch traced here: 93.4 us
  Pallas kernels  92.7 us (99%)
    pallas_call x1, Pallas kernels, backward(): pl.pallas_call(kernel, out_shape=[jax.ShapeDtypeStruct((ROWS, COLS), BF16...  91.1 us

profile of v7, /device:TPU:1, one launch (start us, length us, event | category | flops | bytes accessed | tf_op | source)
XLA Modules:
  0.0 93.4 jit_solution(8315931464337717077)
XLA Ops:
  0.6 91.1 %vicreg_backward.1 = (bf16[128,512]{1,0:T(8,128)(2,1)}, bf16[128,512]{1,0:T(8,128)(2,1)}) custom-call(bf16[128,512]{1,0:T(8,128)(2,1)} %fv.1, bf16[128,512]{1,0:T(8,128)(2,1)} %sv.1, bf16[8,512,512]{2,1,0:T(8,128)(2,1)} %bitcast.1, bf16[128,512]{1,0:T(8,128)(2,1)} %pa.1), custom_call_target="tpu_custom_call" | custom-call | flops 2700000000 | bytes 5000000 | tf_op jit(solution)/shard_map/vicreg_backward/pallas_call | solution.py:435
  91.7 1.7 %store.1 = (bf16[128,512]{1,0:T(8,128)(2,1)}, bf16[128,512]{1,0:T(8,128)(2,1)}) custom-call(bf16[128,512]{1,0:T(8,128)(2,1)} %get-tuple-element.4.a, bf16[128,512]{1,0:T(8,128)(2,1)} %get-tuple-element.5.b), custom_call_target="tpu_custom_call" | custom-call | tf_op jit(solution)/shard_map/store/pallas_call | solution.py:489

commit v8 on v7

--- a/solution.py
+++ b/solution.py
@@ -204,17 +204,16 @@
             held, land = rs_s.at[i, way, k - 1], rs_r.at[i, way, k - 1]
             if k == 2:
                 rs[i, way, 4].wait_recv()
-            if k < 3:
-                rs[i, way, k + 1].wait_recv()
+                rs[i, way, 3].wait_recv()
             for h in range(2):
                 val = cf[i, at, h]
                 if k == 2 and h == way:
                     val = val + rs_r[i, way, 3, h].astype(F32)
-                if k < 3:
-                    val = val + rs_r[i, way, k, h].astype(F32)
+                if k == 2:
+                    val = val + rs_r[i, way, 2, h].astype(F32)
                 rs_s[i, way, k - 1, h] = val.astype(BF16)
         cp = remote(held, land, rsz_ss.at[i, way, k - 1], rsz_rs.at[i, way, k - 1],
-                    along(way, 2 if k == 4 else 1))
+                    along(way, 1 if k % 2 else 2))
         cp.start()
         rs[i, way, k] = cp
         sent.append(cp)
@@ -229,8 +228,11 @@
     def swap_out(i):
         for way in range(2):
             rs[i, way, 1].wait_recv()
+            rs[i, way, 2].wait_recv()
         for h in range(2):
-            mine = cf[i, z, h] + rs_r[i, 0, 0, h].astype(F32) + rs_r[i, 1, 0, h].astype(F32)
+            mine = cf[i, z, h]
+            for way in range(2):
+                mine = mine + rs_r[i, way, 0, h].astype(F32) + rs_r[i, way, 1, h].astype(F32)
             cf[i, z, h] = mine
             yh_s[i, h] = mine.astype(BF16)
         cp = remote(yh_s.at[i], yh_r.at[i], yh_ss.at[i], yh_rs.at[i], to_zy(8))
@@ -241,13 +243,15 @@
     ag = {}
 
     def gather_step(i, way, k):
-        if k in (2, 4):
-            ag[i, way, k // 2].wait_recv()
-        held = call.at[i, unit(1 - way, min(k, 3) - 1)]
         if k == 4:
+            ag[i, way, 2].wait_recv()
             held = call.at[i, unit(1 - way, 2), way]
+        elif k == 3:
+            held = call.at[i, unit(1 - way, 2)]
+        else:
+            held = call.at[i, z]
         cp = remote(held, held, ag_ss.at[i, way, k - 1], ag_rs.at[i, way, k - 1],
-                    along(way, 2 if k == 4 else 1))
+                    along(way, 1 if k % 2 else 2))
         cp.start()
         ag[i, way, k] = cp
         sent.append(cp)
@@ -257,7 +261,7 @@
         for h in range(2):
             full = cf[i, z, h] + yh_r[i, h].astype(F32) + corr[h, z, :, cols[i]]
             call[i, z, h] = full.astype(BF16)
-        gather_all(i, 1)
+        gather_all(i, 2, 1)
 
     def gather_all(i, *steps):
         for k in steps:
@@ -266,6 +270,7 @@
 
     def gather_wait(i):
         for way in range(2):
+            ag[i, way, 1].wait_recv()
             ag[i, way, 3].wait_recv()
             ag[i, way, 4].wait_recv()
 
@@ -274,7 +279,7 @@
     block(0, 0)
     share[0].wait_recv()
     block(0, 1)
-    reduce_all(0, 4, 3)
+    reduce_all(0, 4, 3, 1)
     centre_k(1)
 
     s2 = [remote(tot, st.at[r], st_ss.at[r], st_rs.at[r], to_zy(r)) for r in range(1, 16)]
@@ -283,12 +288,10 @@
     block(1, 0)
     share[1].wait_recv()
     block(1, 1)
-    reduce_all(1, 4, 3)
+    reduce_all(1, 4, 3, 1)
     reduce_all(0, 2)
-    reduce_all(0, 1)
+    swap_out(0)
     reduce_all(1, 2)
-    swap_out(0)
-    reduce_all(1, 1)
 
     for cp in s2:
         cp.wait_recv()
@@ -332,10 +335,8 @@
             for b in range(4):
                 pk[h, i, b] = (pk[h, i, b].astype(F32) + shift[:, cols[i]]).astype(BF16)
     gather_first(0)
-    gather_all(0, 2)
     gather_first(1)
     gather_all(0, 4, 3)
-    gather_all(1, 2)
     gather_all(1, 4, 3)
 
     cx = {}
@@ -355,70 +356,76 @@
     gather_wait(1)
     for q in range(2):
         cov[q] += product(1, q)
+    halves = (slice(0, ROWS // 2), slice(ROWS // 2, ROWS))
+    for i in range(2):
         for r in (2, 1, 3):
-            cx_s[q, r] = cov[q, (x + r) % 4].astype(BF16)
-            cp = remote(cx_s.at[q, r], cx_r.at[q, r], cx_ss.at[q, r], cx_rs.at[q, r], to_x(r))
+            for q in range(2):
+                cx_s[i, r, :, cols[q]] = cov[q, (x + r) % 4, halves[i]].astype(BF16)
+            cp = remote(cx_s.at[i, r], cx_r.at[i, r], cx_ss.at[i, r], cx_rs.at[i, r], to_x(r))
             cp.start()
-            cx[q, r] = cp
+            cx[i, r] = cp
             sent.append(cp)
 
     load_s.wait()
     factor = N * D / loss_share
     vgc = []
 
-    def view_grad(q):
-        at = slice(q * HALF, (q + 1) * HALF)
-        cov_prod = cov[q, x]
+    def view_grad(i):
+        rows = halves[i]
         for r in range(1, 4):
-            cx[q, r].wait_recv()
-            cov_prod = cov_prod + cx_r[q, r].astype(F32)
-        values = xj[x, :, at].astype(F32)
-        centered = values - mean_j[:, at]
-        invariance = 2.0 * inv_weight / (N * D) * (values - svb[:, at].astype(F32))
-        spread_term = -var_weight / D * hinge[:, at] * centered / ((N - 1) * deviation[:, at])
-        cov_term = 4.0 * cov_weight / (D * (N - 1)) * (cov_prod / (N - 1) - centered * variance[:, at])
-        vgs[q] = (factor * (invariance + spread_term + cov_term)).astype(BF16)
-        cp = remote(vgs.at[q], vgp.at[q], vg_ss.at[q], vg_rs.at[q], partner)
+            cx[i, r].wait_recv()
+        for q in range(2):
+            at = cols[q]
+            cov_prod = cov[q, x, rows]
+            for r in range(1, 4):
+                cov_prod = cov_prod + cx_r[i, r, :, at].astype(F32)
+            values = xj[x, rows, at].astype(F32)
+            centered = values - mean_j[:, at]
+            invariance = 2.0 * inv_weight / (N * D) * (values - svb[rows, at].astype(F32))
+            spread_term = -var_weight / D * hinge[:, at] * centered / ((N - 1) * deviation[:, at])
+            cov_term = 4.0 * cov_weight / (D * (N - 1)) * (
+                cov_prod / (N - 1) - centered * variance[:, at])
+            vgs[i, :, at] = (factor * (invariance + spread_term + cov_term)).astype(BF16)
+        cp = remote(vgs.at[i], vgp.at[i], vg_ss.at[i], vg_rs.at[i], partner)
         cp.start()
         vgc.append(cp)
         sent.append(cp)
 
-    view_grad(0)
-    view_grad(1)
-
     bk = []
 
-    def back(r):
+    def back(i, r):
         at = (yl + r) % 4
-        out = None
-        for core, held in enumerate((vgs, vgp)):
-            for q in range(2):
-                if core == 1 and r == 2:
-                    vgc[q].wait_recv()
-                part = lax.dot_general(held[q], wb[at, core, :, cols[q]], NT, preferred_element_type=F32)
-                out = part if out is None else out + part
-        return out
+        out = lax.dot_general(vgs[i], wb[at, 0], NT, preferred_element_type=F32)
+        if r == 2:
+            vgc[i].wait_recv()
+        return out + lax.dot_general(vgp[i], wb[at, 1], NT, preferred_element_type=F32)
+
+    def send_back(i):
+        for r in (2, 1, 3):
+            bk_s[i, r] = back(i, r).astype(BF16)
+            cp = remote(bk_s.at[i, r], bk_r.at[i, r], bk_ss.at[i, r], bk_rs.at[i, r], to_yl(r))
+            cp.start()
+            bk.append(cp)
+            sent.append(cp)
 
     for cp in load_w:
         cp.wait()
     for cp in lend_w:
         cp.wait_recv()
-    for r in (2, 1, 3):
-        bk_s[r] = back(r).astype(BF16)
-        cp = remote(bk_s.at[r], bk_r.at[r], bk_ss.at[r], bk_rs.at[r], to_yl(r))
-        cp.start()
-        bk.append(cp)
-        sent.append(cp)
-    keep[...] = back(0)
-    for q in range(2):
-        vg_out[:, cols[q]] = vgs[q]
+    for i in range(2):
+        view_grad(i)
+        send_back(i)
     load_p.wait()
+    for i in range(2):
+        vg_out[halves[i]] = vgs[i]
+        keep[halves[i]] = back(i, 0)
     for cp in bk:
         cp.wait_recv()
-    total = keep[...]
-    for r in range(1, 4):
-        total = total + bk_r[r].astype(F32)
-    pg_out[...] = jnp.where(pab[...] > 0, total, 0.0).astype(BF16)
+    for i in range(2):
+        total = keep[halves[i]]
+        for r in range(1, 4):
+            total = total + bk_r[i, r].astype(F32)
+        pg_out[halves[i]] = jnp.where(pab[halves[i]] > 0, total, 0.0).astype(BF16)
 
     for cp in gj + gk[0][1:] + gk[1][1:] + s2 + [share_d] + lend_w + sent:
         cp.wait_send()
@@ -459,18 +466,18 @@
             vmem((2, 2, UNIT, HALF), BF16),
             vmem((2, 8, 2, UNIT, HALF), BF16),
             vmem((2, 4, ROWS, HALF), F32),
-            vmem((2, 4, ROWS, HALF), BF16),
-            vmem((2, 4, ROWS, HALF), BF16),
-            vmem((2, ROWS, HALF), BF16),
-            vmem((2, ROWS, HALF), BF16),
-            vmem((4, ROWS, COLS), BF16),
-            vmem((4, ROWS, COLS), BF16),
+            vmem((2, 4, ROWS // 2, COLS), BF16),
+            vmem((2, 4, ROWS // 2, COLS), BF16),
+            vmem((2, ROWS // 2, COLS), BF16),
+            vmem((2, ROWS // 2, COLS), BF16),
+            vmem((2, 4, ROWS // 2, COLS), BF16),
+            vmem((2, 4, ROWS // 2, COLS), BF16),
             vmem((ROWS, COLS), F32),
             dma((6,)),
             dma((4,)), dma((4,)), dma((2, 4)), dma((2, 4)), dma((16,)), dma((16,)), dma, dma,
             dma((2,)), dma((2,)), dma((2, 2, 4)), dma((2, 2, 4)), dma((2,)), dma((2,)),
             dma((2, 2, 4)), dma((2, 2, 4)),
-            dma((2, 4)), dma((2, 4)), dma((2,)), dma((2,)), dma((4,)), dma((4,)),
+            dma((2, 4)), dma((2, 4)), dma((2,)), dma((2,)), dma((2, 4)), dma((2, 4)),
             dma((4,)), dma((4,)), dma((4,)),
         ],
         compiler_params=pltpu.CompilerParams(

time: 93.8 us -> 93.2 us (level)
  no operation moved by 1% of the time
where the time goes in v8:
time: 93.2 us; the launch traced here: 93 us
  Pallas kernels  92.4 us (99%)
    pallas_call x1, Pallas kernels, backward(): pl.pallas_call(kernel, out_shape=[jax.ShapeDtypeStruct((ROWS, COLS), BF16...  90.7 us

profile of v8, /device:TPU:1, one launch (start us, length us, event | category | flops | bytes accessed | tf_op | source)
XLA Modules:
  0.0 93.0 jit_solution(10285935627497975208)
XLA Ops:
  0.6 90.7 %vicreg_backward.1 = (bf16[128,512]{1,0:T(8,128)(2,1)}, bf16[128,512]{1,0:T(8,128)(2,1)}) custom-call(bf16[128,512]{1,0:T(8,128)(2,1)} %fv.1, bf16[128,512]{1,0:T(8,128)(2,1)} %sv.1, bf16[8,512,512]{2,1,0:T(8,128)(2,1)} %bitcast.1, bf16[128,512]{1,0:T(8,128)(2,1)} %pa.1), custom_call_target="tpu_custom_call" | custom-call | flops 2700000000 | bytes 5000000 | tf_op jit(solution)/shard_map/vicreg_backward/pallas_call | solution.py:442
  91.3 1.7 %store.1 = (bf16[128,512]{1,0:T(8,128)(2,1)}, bf16[128,512]{1,0:T(8,128)(2,1)}) custom-call(bf16[128,512]{1,0:T(8,128)(2,1)} %get-tuple-element.4.a, bf16[128,512]{1,0:T(8,128)(2,1)} %get-tuple-element.5.b), custom_call_target="tpu_custom_call" | custom-call | tf_op jit(solution)/shard_map/store/pallas_call | solution.py:496

commit v9 on v8

--- a/solution.py
+++ b/solution.py
@@ -56,10 +56,11 @@
     def to_yl(r):
         return dev(z, yh, x, (yl + r) % 4, c)
 
-    def to_zy(r):
-        return dev((z + r % 8) % 8, (yh + r // 8) % 2, x, yl, c)
+    def to_z(r):
+        return dev((z + r) % 8, yh, x, yl, c)
 
     partner = dev(z, yh, x, yl, 1 - c)
+    across = dev(z, 1 - yh, x, yl, c)
     diagonal = x == yl
 
     def remote(src, dst, ss, rs, to):
@@ -84,9 +85,11 @@
         pl.semaphore_signal(barrier, inc=1, device_id=to, device_id_type=pl.DeviceIdType.MESH)
 
     count = 0
-    for r in range(1, 16):
-        greet(to_zy(r))
+    for r in range(1, 8):
+        greet(to_z(r))
         count += 1
+    greet(across)
+    count += 1
     for r in range(1, 4):
         greet(to_x(r))
         greet(to_k(r))
@@ -235,7 +238,7 @@
                 mine = mine + rs_r[i, way, 0, h].astype(F32) + rs_r[i, way, 1, h].astype(F32)
             cf[i, z, h] = mine
             yh_s[i, h] = mine.astype(BF16)
-        cp = remote(yh_s.at[i], yh_r.at[i], yh_ss.at[i], yh_rs.at[i], to_zy(8))
+        cp = remote(yh_s.at[i], yh_r.at[i], yh_ss.at[i], yh_rs.at[i], across)
         cp.start()
         swap[i] = cp
         sent.append(cp)
@@ -282,7 +285,7 @@
     reduce_all(0, 4, 3, 1)
     centre_k(1)
 
-    s2 = [remote(tot, st.at[r], st_ss.at[r], st_rs.at[r], to_zy(r)) for r in range(1, 16)]
+    s2 = [remote(tot, st.at[r], st_ss.at[r], st_rs.at[r], to_z(r)) for r in range(1, 8)]
     for cp in s2:
         cp.start()
     block(1, 0)
@@ -290,19 +293,23 @@
     block(1, 1)
     reduce_all(1, 4, 3, 1)
     reduce_all(0, 2)
-    swap_out(0)
-    reduce_all(1, 2)
-
+    st[0] = tot[...]
     for cp in s2:
         cp.wait_recv()
-    sums = tot[...]
+    s2.append(remote(st.at[pl.ds(0, 8)], st.at[pl.ds(8, 8)], st_ss.at[8], st_rs.at[8], across))
+    s2[-1].start()
+    reduce_all(1, 2)
+    swap_out(0)
+    swap_out(1)
+
+    s2[-1].wait_recv()
+    sums = st[0]
     for r in range(1, 16):
         sums = sums + st[r]
     mean_j, mean_k = sums[0] / N, sums[2] / N
     for r in range(16):
-        own = tot[...] if r == 0 else st[r]
-        dsj[r:r + 1, :] = own[0] / GROUP - mean_j
-        dsk[r:r + 1, :] = own[2] / GROUP - mean_k
+        dsj[r:r + 1, :] = st[r, 0] / GROUP - mean_j
+        dsk[r:r + 1, :] = st[r, 2] / GROUP - mean_k
     gap_j, gap_k = dsj[...], dsk[...]
     variance = (sums[1] + GROUP * jnp.sum(gap_j * gap_j, axis=0, keepdims=True)) / (N - 1)
     deviation = jnp.sqrt(variance + var_eps)
@@ -323,10 +330,13 @@
         corr[h] = lax.dot_general(
             dja[...], dkb[h], TN, preferred_element_type=F32).reshape(8, UNIT, COLS)
 
-    swap_out(1)
     correction(0)
     share_d.wait_recv()
     correction(1)
+
+    gather_first(0)
+    gather_first(1)
+    gather_all(0, 4, 3)
 
     for i in range(2):
         share[i].wait_send()
@@ -334,9 +344,6 @@
             shift = dkb[h, 0:16].astype(F32)[0:1] + dkb[h, 16:32].astype(F32)[0:1]
             for b in range(4):
                 pk[h, i, b] = (pk[h, i, b].astype(F32) + shift[:, cols[i]]).astype(BF16)
-    gather_first(0)
-    gather_first(1)
-    gather_all(0, 4, 3)
     gather_all(1, 4, 3)
 
     cx = {}

time: 93.2 us -> 89.5 us (0.960)
  Pallas kernels: 92.4 us -> 88.7 us
    pallas_call x1, Pallas kernels: 90.7 us -> 87 us  [backward(): pl.pallas_call(kernel, out_shape=[jax.ShapeDtypeStruct((ROWS, COLS), BF16...]
where the time goes in v9:
time: 89.5 us; the launch traced here: 89.3 us
  Pallas kernels  88.7 us (99%)
    pallas_call x1, Pallas kernels, backward(): pl.pallas_call(kernel, out_shape=[jax.ShapeDtypeStruct((ROWS, COLS), BF16...  87 us

profile of v9, /device:TPU:1, one launch (start us, length us, event | category | flops | bytes accessed | tf_op | source)
XLA Modules:
  0.0 89.3 jit_solution(13949419803509540089)
XLA Ops:
  0.6 87.0 %vicreg_backward.1 = (bf16[128,512]{1,0:T(8,128)(2,1)}, bf16[128,512]{1,0:T(8,128)(2,1)}) custom-call(bf16[128,512]{1,0:T(8,128)(2,1)} %fv.1, bf16[128,512]{1,0:T(8,128)(2,1)} %sv.1, bf16[8,512,512]{2,1,0:T(8,128)(2,1)} %bitcast.1, bf16[128,512]{1,0:T(8,128)(2,1)} %pa.1), custom_call_target="tpu_custom_call" | custom-call | flops 2700000000 | bytes 5000000 | tf_op jit(solution)/shard_map/vicreg_backward/pallas_call | solution.py:449
  87.6 1.7 %store.1 = (bf16[128,512]{1,0:T(8,128)(2,1)}, bf16[128,512]{1,0:T(8,128)(2,1)}) custom-call(bf16[128,512]{1,0:T(8,128)(2,1)} %get-tuple-element.4.a, bf16[128,512]{1,0:T(8,128)(2,1)} %get-tuple-element.5.b), custom_call_target="tpu_custom_call" | custom-call | tf_op jit(solution)/shard_map/store/pallas_call | solution.py:503

commit v10 on v9

--- a/solution.py
+++ b/solution.py
@@ -84,25 +84,22 @@
     def greet(to):
         pl.semaphore_signal(barrier, inc=1, device_id=to, device_id_type=pl.DeviceIdType.MESH)
 
-    count = 0
-    for r in range(1, 8):
-        greet(to_z(r))
-        count += 1
-    greet(across)
-    count += 1
-    for r in range(1, 4):
-        greet(to_x(r))
-        greet(to_k(r))
-        greet(from_k(r))
-        greet(to_yl(r))
-        count += 4
-    greet(partner)
-    count += 1
-
     @pl.when(jnp.logical_not(diagonal))
     def _():
         greet(to_k(0))
         greet(from_k(0))
+
+    for r in range(1, 4):
+        greet(to_k(r))
+        greet(from_k(r))
+    greet(across)
+    for r in (4, 3, 5, 2, 6, 1, 7):
+        greet(to_z(r))
+    for r in range(1, 4):
+        greet(to_yl(r))
+        greet(to_x(r))
+    greet(partner)
+    count = 21
 
     @pl.when(diagonal)
     def _():
@@ -494,17 +491,25 @@
     )(first_view, second_view, weight.reshape(8, COLS, COLS), pre_act)
 
 
-def store_kernel(a, b, a_out, b_out):
-    a_out[...] = a[...]
-    b_out[...] = b[...]
+def store_kernel(a, b, a_out, b_out, held, sems):
+    first = [pltpu.make_async_copy(src, held.at[i], sems.at[0, i]) for i, src in enumerate((a, b))]
+    second = [pltpu.make_async_copy(held.at[i], dst, sems.at[1, i]) for i, dst in enumerate((a_out, b_out))]
+    for cp in first:
+        cp.start()
+    for load, store in zip(first, second):
+        load.wait()
+        store.start()
+    for cp in second:
+        cp.wait()
 
 
 def on_device(*args):
     return pl.pallas_call(
         store_kernel,
         out_shape=[jax.ShapeDtypeStruct((ROWS, COLS), BF16)] * 2,
-        in_specs=[pl.BlockSpec(memory_space=pltpu.VMEM)] * 2,
-        out_specs=[pl.BlockSpec(memory_space=pltpu.VMEM)] * 2,
+        in_specs=[pl.BlockSpec(memory_space=pl.ANY)] * 2,
+        out_specs=[pl.BlockSpec(memory_space=pl.ANY)] * 2,
+        scratch_shapes=[pltpu.VMEM((2, ROWS, COLS), BF16), pltpu.SemaphoreType.DMA((2, 2))],
         compiler_params=pltpu.CompilerParams(vmem_limit_bytes=60 * 2**20),
         name="store",
     )(*backward(*args))

time: 89.5 us -> 89.6 us (level)
  no operation moved by 1% of the time
where the time goes in v10:
time: 89.6 us; the launch traced here: 89.4 us
  Pallas kernels  88.8 us (99%)
    pallas_call x1, Pallas kernels, backward(): pl.pallas_call(kernel, out_shape=[jax.ShapeDtypeStruct((ROWS, COLS), BF16...  87.1 us

profile of v10, /device:TPU:1, one launch (start us, length us, event | category | flops | bytes accessed | tf_op | source)
XLA Modules:
  0.0 89.4 jit_solution(17209368784539267521)
XLA Ops:
  0.6 87.1 %vicreg_backward.1 = (bf16[128,512]{1,0:T(8,128)(2,1)}, bf16[128,512]{1,0:T(8,128)(2,1)}) custom-call(bf16[128,512]{1,0:T(8,128)(2,1)} %fv.1, bf16[128,512]{1,0:T(8,128)(2,1)} %sv.1, bf16[8,512,512]{2,1,0:T(8,128)(2,1)} %bitcast.1, bf16[128,512]{1,0:T(8,128)(2,1)} %pa.1), custom_call_target="tpu_custom_call" | custom-call | flops 2700000000 | bytes 5000000 | tf_op jit(solution)/shard_map/vicreg_backward/pallas_call | solution.py:446
  87.7 1.7 %store.1 = (bf16[128,512]{1,0:T(8,128)(2,1)}, bf16[128,512]{1,0:T(8,128)(2,1)}) custom-call(bf16[128,512]{1,0:T(8,128)(2,1)} %get-tuple-element.4.a, bf16[128,512]{1,0:T(8,128)(2,1)} %get-tuple-element.5.b), custom_call_target="tpu_custom_call" | custom-call | tf_op jit(solution)/shard_map/store/pallas_call | solution.py:507
